TPU v7x, 128 devices: a whole 4x4x4 slice. The times are simulated.
128 devices in a mesh: angle: 8 (over x, y_lo), row: 16 (over z, y_hi, core).
Axes of the slice: x: 4, y: 4 (y_hi: 2, y_lo: 2; y = y_hi * 2 + y_lo), z: 4, core: 2. Of those that a mesh axis runs over, the one named last changes fastest.
Arguments:
- hologram: bfloat16 [16, 2048, 2048], P('angle', 'row'), may hold values from -6 to 6
- centres: int32 [16, 2], P('angle'), may hold values from 256 to 767
- offsets: int32 [16, 16, 16], P('angle', 'row'), may hold values from -1 to 1
- angle_index: int32 [16], replicated, may hold values from 0 to 1199
Outputs:
- volume: float32 [8, 1024, 1024], P('angle', 'row')
Inputs may be any that keep to these rules, and one draw needn't show every extreme that they name: `angle_index`: angle indices into the scan of 1200 angles.
All inputs are finite; a program needn't handle non-finite values.
Results may differ from a plain program's by a relative error of at most 0.02.
Values may be sent and summed in bfloat16 or wider, within the bound.
A program may use at most 192 MiB of HBM per device.

v0:
```python
import math

import jax
import jax.numpy as jnp
from jax import lax
from jax.sharding import PartitionSpec as P

PIX = 2048
CROP = 1024
BLOCK = 64
PLANES = 8
ANGLES = 1200


full_turn = 2.0 * math.pi
wave_number = 4.0


def turn_table(left_ints, right_ints, period):
    product = jnp.mod(left_ints[:, None] * right_ints[None, :], period)
    angles = product.astype(jnp.float32) * jnp.float32(full_turn / period)
    factor = jnp.float32(1.0 / math.sqrt(period))
    return (
        (jnp.cos(angles) * factor).astype(jnp.bfloat16),
        (jnp.sin(angles) * factor).astype(jnp.bfloat16),
    )


def angle_trig(angle_at):
    tilt_angle = angle_at.astype(jnp.float32) * jnp.float32(full_turn / ANGLES)
    return (jnp.cos(tilt_angle), jnp.sin(tilt_angle))


def plane_kernel(cosine, sine_value, depth_at, holo_count):
    shifted = jnp.arange(CROP, dtype=jnp.int32) - CROP // 2
    spatial = shifted.astype(jnp.float32) * jnp.float32(full_turn / CROP)
    lateral = shifted.astype(jnp.float32)
    along_axis = lateral * cosine + depth_at * sine_value
    depth_axis = depth_at * cosine - lateral * sine_value
    axial = jnp.sqrt(wave_number * wave_number - spatial * spatial) - wave_number
    phases = spatial[:, None] * along_axis[None, :] + axial[:, None] * depth_axis[None, :]
    weight = jnp.abs(spatial) / jnp.float32(math.pi * math.sqrt(CROP * holo_count))
    real_part = (weight[:, None] * jnp.cos(phases)).astype(jnp.bfloat16)
    imag_part = (weight[:, None] * jnp.sin(phases)).astype(jnp.bfloat16)
    return jnp.concatenate([real_part, imag_part], axis=0)


def mat(left, right):
    return jnp.dot(left, right, preferred_element_type=jnp.float32)


def contract_first(left, right):
    return lax.dot_general(
        left, right, (((0,), (0,)), ((), ())), preferred_element_type=jnp.float32
    )


def per_device(hologram, centres, offsets, angle_index):
    held = hologram.shape[0]
    row_height = hologram.shape[1]
    groups = lax.axis_size("angle")
    total_holos = held * groups
    per_dev = PLANES // groups
    pixels = jnp.arange(PIX, dtype=jnp.int32)
    freq_bins = jnp.arange(CROP, dtype=jnp.int32)
    columns = []
    for member in range(held):
        cols_cos, cols_sin = turn_table(pixels, centres[member, 0] - CROP // 2 + freq_bins, PIX)
        stacked = jnp.concatenate([cols_cos, -cols_sin], axis=1)
        spectra = lax.dot_general(
            stacked, hologram[member], (((0,), (1,)), ((), ())), preferred_element_type=jnp.float32
        )
        columns.append(spectra.astype(jnp.bfloat16).reshape(2, CROP, row_height))
    outgoing = jnp.stack(columns)
    incoming = lax.all_to_all(outgoing, "row", split_axis=2, concat_axis=3, tiled=True)
    back_cos, back_sin = turn_table(freq_bins - CROP // 2, freq_bins, CROP)
    inverse = jnp.concatenate([back_cos, back_sin], axis=1)
    middles = []
    for member in range(held):
        rows_cos, rows_sin = turn_table(pixels, centres[member, 1] - CROP // 2 + freq_bins, PIX)
        forward = jnp.concatenate([rows_cos, rows_sin], axis=1)
        prod_one = mat(incoming[member, 0], forward)
        prod_two = mat(incoming[member, 1], forward)
        spec_real = (prod_one[:, :CROP] + prod_two[:, CROP:]).astype(jnp.bfloat16)
        spec_imag = (prod_two[:, :CROP] - prod_one[:, CROP:]).astype(jnp.bfloat16)
        prod_three = mat(spec_real, inverse)
        prod_four = mat(spec_imag, inverse)
        mid_real = prod_three[:, :CROP] - prod_four[:, CROP:]
        mid_imag = prod_three[:, CROP:] + prod_four[:, :CROP]
        middles.append(jnp.stack([mid_real, mid_imag]).astype(jnp.bfloat16))
    middle = jnp.stack(middles)
    returned = lax.all_to_all(middle, "row", split_axis=3, concat_axis=2, tiled=True)
    wave_cos, wave_sin = turn_table(freq_bins - CROP // 2, freq_bins - CROP // 2, CROP)
    wave_table = jnp.concatenate([wave_cos, wave_sin], axis=1)
    filter_list = []
    for member in range(held):
        prod_five = contract_first(returned[member, 0], inverse)
        prod_six = contract_first(returned[member, 1], inverse)
        field_real = prod_five[:, :CROP] - prod_six[:, CROP:]
        field_imag = prod_five[:, CROP:] + prod_six[:, :CROP]
        energy = field_real * field_real + field_imag * field_imag + 1.0
        magnitude = jnp.sqrt(energy)
        unwrap = jnp.repeat(jnp.repeat(offsets[member], BLOCK, axis=0), BLOCK, axis=1).astype(
            jnp.float32
        )
        ry_real = (0.5 * jnp.log(energy)).astype(jnp.bfloat16)
        ry_imag = (
            2.0 * jnp.arctan(field_imag / (magnitude + jnp.abs(field_real))) + full_turn * unwrap
        ).astype(jnp.bfloat16)
        prod_seven = mat(ry_real, wave_table)
        prod_eight = mat(ry_imag, wave_table)
        filt_real = (prod_seven[:, :CROP] + prod_eight[:, CROP:]).astype(jnp.bfloat16)
        filt_imag = (prod_eight[:, :CROP] - prod_seven[:, CROP:]).astype(jnp.bfloat16)
        filter_list.append(jnp.concatenate([filt_real, -filt_imag], axis=1))
    filters = jnp.stack(filter_list)
    slab = filters.shape[1]
    first_plane = lax.axis_index("angle") * per_dev
    empty_sum = jnp.zeros((per_dev, slab, CROP), jnp.float32)
    arriving = lax.all_gather(filters, "angle", axis=0, tiled=True)

    def add_one(position, running):
        angle_at = lax.dynamic_index_in_dim(angle_index, position, 0, keepdims=False)
        cosine, sine_value = angle_trig(angle_at)
        filt_rows = lax.dynamic_index_in_dim(arriving, position, 0, keepdims=False)
        depth_at = (first_plane + 0 - PLANES // 2).astype(jnp.float32)
        slices_list = [mat(filt_rows, plane_kernel(cosine, sine_value, depth_at, total_holos))]
        return running + jnp.stack(slices_list)

    return lax.fori_loop(0, arriving.shape[0], add_one, empty_sum)


def solution(mesh):
    placed = (P("angle", "row", None), P("angle", None), P("angle", "row", None), P())
    return jax.shard_map(
        per_device, mesh=mesh, in_specs=placed, out_specs=P("angle", "row", None), check_vma=False
    )
```

profile of v0, /device:TPU:8, one launch (start us, length us, event | category | flops | bytes accessed | tf_op | source)
XLA Modules:
  0.0 742.5 jit_solution(16083950101668113330)
XLA Ops:
  6.5 1.4 fusion.129
  8.6 31.7 %fusion.56 = bf16[2048,1024]{1,0:T(8,128)(2,1)S(1)} fusion(s32[1024]{0:T(1024)S(1)} %iota_add_fusion.5), kind=kLoop, calls=%fused_computation.91 | loop fusion | flops 39845888 | bytes 4198400 | tf_op jit(solution)/shard_map/neg | solution.py:69
  40.3 31.4 %multiply_convert_fusion.9 = bf16[2048,1024]{1,0:T(8,128)(2,1)S(1)} fusion(s32[1024]{0:T(1024)S(1)} %iota_add_fusion.5), kind=kLoop, calls=%fused_computation.66 | loop fusion | flops 33554432 | bytes 4198400 | tf_op jit(solution)/shard_map/convert_element_type | solution.py:24
  72.4 31.7 %fusion.57 = bf16[2048,1024]{1,0:T(8,128)(2,1)S(1)} fusion(s32[1024]{0:T(1024)S(1)} %iota_add_fusion.4), kind=kLoop, calls=%fused_computation.92 | loop fusion | flops 39845888 | bytes 4198400 | tf_op jit(solution)/shard_map/neg | solution.py:69
  104.1 31.9 %multiply_convert_fusion.7 = bf16[2048,1024]{1,0:T(8,128)(2,1)S(1)} fusion(s32[1024]{0:T(1024)S(1)} %iota_add_fusion.4), kind=kLoop, calls=%fused_computation.62 | loop fusion | flops 33554432 | bytes 4198400 | tf_op jit(solution)/shard_map/convert_element_type | solution.py:24
  136.0 2.4 fusion.64
  139.0 2.4 fusion.61
  142.0 2.5 pad_maximum_fusion.8
  144.6 7.3 all-to-all-start
  152.5 35.3 %multiply_convert_fusion.3 = (bf16[2048,1024]{1,0:T(8,128)(2,1)}, bf16[2048,1024]{1,0:T(8,128)(2,1)}) fusion(s32[1024]{0:T(1024)S(1)} %iota_add_fusion.1), kind=kLoop, calls=%fused_computation.54 | loop fusion | flops 37748736 | bytes 8392704 | tf_op jit(solution)/shard_map/convert_element_type | solution.py:24
  187.8 36.3 %multiply_convert_fusion.11 = (bf16[1024,1024]{1,0:T(8,128)(2,1)}, bf16[1024,1024]{1,0:T(8,128)(2,1)S(1)}, bf16[1024,1024]{1,0:T(8,128)(2,1)}, bf16[1024,1024]{1,0:T(8,128)(2,1)}) fusion(s32[1024]{0:T(1024)S(1)} %iota_add_fusion.2), kind=kLoop, calls=%fused_computation.96 | loop fusion | flops 37748736 | bytes 8392704 | tf_op jit(solution)/shard_map/convert_element_type | solution.py:24
  224.8 35.3 %multiply_convert_fusion.5 = (bf16[2048,1024]{1,0:T(8,128)(2,1)}, bf16[2048,1024]{1,0:T(8,128)(2,1)}) fusion(s32[1024]{0:T(1024)S(1)} %iota_add_fusion.3), kind=kLoop, calls=%fused_computation.58 | loop fusion | flops 37748736 | bytes 8392704 | tf_op jit(solution)/shard_map/convert_element_type | solution.py:24
  260.6 1.7 copy-done
  262.3 4.3 fusion.46
  266.7 1.6 fusion.47
  269.1 0.8 fusion.95
  270.5 1.5 copy-done.2
  272.0 1.6 fusion.48
  273.5 1.6 fusion.49
  277.9 1.5 reshape.152
  279.4 7.3 all-to-all-start.1
  287.4 11.8 %all-to-all-done.1 = bf16[16,2,8192]{2,1,0:T(2,128)(2,1)S(1)} async-done(((bf16[16,2,8192]{2,1,0:T(2,128)(2,1)}), bf16[16,2,8192]{2,1,0:T(2,128)(2,1)S(1)}, u32[]{:S(2)}, u32[]{:S(2)}) %all-to-all-start.1) | async-done | bytes 524320 | tf_op jit(solution)/shard_map/all_to_all | solution.py:92
  301.2 3.2 fusion.104
  306.9 0.9 fusion.83
  307.8 1.2 fusion.84
  309.1 0.8 fusion.102
  309.9 0.8 fusion.101
  310.8 0.8 fusion.85
  311.6 1.2 fusion.86
  313.0 0.9 pad_maximum_fusion.9
  313.9 86.2 %all-gather.2.cloned.1.call-done = bf16[16,64,2048]{2,1,0:T(8,128)(2,1)} async-done(((bf16[2,64,2048]{2,1,0:T(8,128)(2,1)}), bf16[16,64,2048]{2,1,0:T(8,128)(2,1)}) %all-gather.2.cloned.1.call-update) | async-done | bytes 4194320 | tf_op jit(solution)/shard_map/all_gather | solution.py:119
  400.1 334.6 %while.16 = (s32[]{:T(128)}, f32[1,64,1024]{2,1,0:T(8,128)S(1)}, bf16[16,64,2048]{2,1,0:T(8,128)(2,1)}, s32[16]{0:T(128)S(1)}, f32[]{:T(128)}, /*index=5*/s32[]{:T(128)}, f32[1]{0:T(128)}, s32[]{:T(128)}) while((s32[]{:T(128)}, f32[1,64,1024]{2,1,0:T(8,128)S(1)}, bf16[16,64,2048]{2,1,0:T(8,128)(2,1)}, s32[16]{0:T(128)S(1)}, ...), condition=%wide.region_1.2_spmd.clone, body=%wide.region_0.1_spmd.clone.sunk | while | flops 284313600 | bytes 9216695 | solution.py:129
  401.4 17.0 %multiply_convert_fusion.19 = (bf16[1024,1024]{1,0:T(8,128)(2,1)S(1)}, bf16[1024,1024]{1,0:T(8,128)(2,1)}) fusion(f32[1024]{0:T(1024)S(1)} %get-tuple-element.234, f32[1024]{0:T(1024)S(1)} %get-tuple-element.235, f32[1024]{0:T(1024)S(1)} %get-tuple-element.236, f32[1024]{0:T(1024)S(1)} %convert_multiply_fusion.2, f32[1024]{0:T(1024)S(1)} %get-tuple-element.237), kind=kLoop, calls=%fused_computation.5.clone.1 | loop fusion | flops 7340032 | bytes 4214784 | tf_op jit(solution)/shard_map/while/body/eval_jaxpr/convert_element_type | solution.py:43
  418.4 2.6 fusion.135
  422.3 17.0 %multiply_convert_fusion.19 = (bf16[1024,1024]{1,0:T(8,128)(2,1)S(1)}, bf16[1024,1024]{1,0:T(8,128)(2,1)}) fusion(f32[1024]{0:T(1024)S(1)} %get-tuple-element.234, f32[1024]{0:T(1024)S(1)} %get-tuple-element.235, f32[1024]{0:T(1024)S(1)} %get-tuple-element.236, f32[1024]{0:T(1024)S(1)} %convert_multiply_fusion.2, f32[1024]{0:T(1024)S(1)} %get-tuple-element.237), kind=kLoop, calls=%fused_computation.5.clone.1 | loop fusion | flops 7340032 | bytes 4214784 | tf_op jit(solution)/shard_map/while/body/eval_jaxpr/convert_element_type | solution.py:43
  439.3 2.6 fusion.135
  443.2 17.0 %multiply_convert_fusion.19 = (bf16[1024,1024]{1,0:T(8,128)(2,1)S(1)}, bf16[1024,1024]{1,0:T(8,128)(2,1)}) fusion(f32[1024]{0:T(1024)S(1)} %get-tuple-element.234, f32[1024]{0:T(1024)S(1)} %get-tuple-element.235, f32[1024]{0:T(1024)S(1)} %get-tuple-element.236, f32[1024]{0:T(1024)S(1)} %convert_multiply_fusion.2, f32[1024]{0:T(1024)S(1)} %get-tuple-element.237), kind=kLoop, calls=%fused_computation.5.clone.1 | loop fusion | flops 7340032 | bytes 4214784 | tf_op jit(solution)/shard_map/while/body/eval_jaxpr/convert_element_type | solution.py:43
  460.2 2.6 fusion.135
  464.2 17.0 %multiply_convert_fusion.19 = (bf16[1024,1024]{1,0:T(8,128)(2,1)S(1)}, bf16[1024,1024]{1,0:T(8,128)(2,1)}) fusion(f32[1024]{0:T(1024)S(1)} %get-tuple-element.234, f32[1024]{0:T(1024)S(1)} %get-tuple-element.235, f32[1024]{0:T(1024)S(1)} %get-tuple-element.236, f32[1024]{0:T(1024)S(1)} %convert_multiply_fusion.2, f32[1024]{0:T(1024)S(1)} %get-tuple-element.237), kind=kLoop, calls=%fused_computation.5.clone.1 | loop fusion | flops 7340032 | bytes 4214784 | tf_op jit(solution)/shard_map/while/body/eval_jaxpr/convert_element_type | solution.py:43
  481.1 2.6 fusion.135
  485.1 17.0 %multiply_convert_fusion.19 = (bf16[1024,1024]{1,0:T(8,128)(2,1)S(1)}, bf16[1024,1024]{1,0:T(8,128)(2,1)}) fusion(f32[1024]{0:T(1024)S(1)} %get-tuple-element.234, f32[1024]{0:T(1024)S(1)} %get-tuple-element.235, f32[1024]{0:T(1024)S(1)} %get-tuple-element.236, f32[1024]{0:T(1024)S(1)} %convert_multiply_fusion.2, f32[1024]{0:T(1024)S(1)} %get-tuple-element.237), kind=kLoop, calls=%fused_computation.5.clone.1 | loop fusion | flops 7340032 | bytes 4214784 | tf_op jit(solution)/shard_map/while/body/eval_jaxpr/convert_element_type | solution.py:43
  502.0 2.6 fusion.135
  506.0 17.0 %multiply_convert_fusion.19 = (bf16[1024,1024]{1,0:T(8,128)(2,1)S(1)}, bf16[1024,1024]{1,0:T(8,128)(2,1)}) fusion(f32[1024]{0:T(1024)S(1)} %get-tuple-element.234, f32[1024]{0:T(1024)S(1)} %get-tuple-element.235, f32[1024]{0:T(1024)S(1)} %get-tuple-element.236, f32[1024]{0:T(1024)S(1)} %convert_multiply_fusion.2, f32[1024]{0:T(1024)S(1)} %get-tuple-element.237), kind=kLoop, calls=%fused_computation.5.clone.1 | loop fusion | flops 7340032 | bytes 4214784 | tf_op jit(solution)/shard_map/while/body/eval_jaxpr/convert_element_type | solution.py:43
  523.0 2.6 fusion.135
  526.9 17.0 %multiply_convert_fusion.19 = (bf16[1024,1024]{1,0:T(8,128)(2,1)S(1)}, bf16[1024,1024]{1,0:T(8,128)(2,1)}) fusion(f32[1024]{0:T(1024)S(1)} %get-tuple-element.234, f32[1024]{0:T(1024)S(1)} %get-tuple-element.235, f32[1024]{0:T(1024)S(1)} %get-tuple-element.236, f32[1024]{0:T(1024)S(1)} %convert_multiply_fusion.2, f32[1024]{0:T(1024)S(1)} %get-tuple-element.237), kind=kLoop, calls=%fused_computation.5.clone.1 | loop fusion | flops 7340032 | bytes 4214784 | tf_op jit(solution)/shard_map/while/body/eval_jaxpr/convert_element_type | solution.py:43
  543.9 2.6 fusion.135
  547.8 17.0 %multiply_convert_fusion.19 = (bf16[1024,1024]{1,0:T(8,128)(2,1)S(1)}, bf16[1024,1024]{1,0:T(8,128)(2,1)}) fusion(f32[1024]{0:T(1024)S(1)} %get-tuple-element.234, f32[1024]{0:T(1024)S(1)} %get-tuple-element.235, f32[1024]{0:T(1024)S(1)} %get-tuple-element.236, f32[1024]{0:T(1024)S(1)} %convert_multiply_fusion.2, f32[1024]{0:T(1024)S(1)} %get-tuple-element.237), kind=kLoop, calls=%fused_computation.5.clone.1 | loop fusion | flops 7340032 | bytes 4214784 | tf_op jit(solution)/shard_map/while/body/eval_jaxpr/convert_element_type | solution.py:43
  564.8 2.6 fusion.135
  568.7 17.0 %multiply_convert_fusion.19 = (bf16[1024,1024]{1,0:T(8,128)(2,1)S(1)}, bf16[1024,1024]{1,0:T(8,128)(2,1)}) fusion(f32[1024]{0:T(1024)S(1)} %get-tuple-element.234, f32[1024]{0:T(1024)S(1)} %get-tuple-element.235, f32[1024]{0:T(1024)S(1)} %get-tuple-element.236, f32[1024]{0:T(1024)S(1)} %convert_multiply_fusion.2, f32[1024]{0:T(1024)S(1)} %get-tuple-element.237), kind=kLoop, calls=%fused_computation.5.clone.1 | loop fusion | flops 7340032 | bytes 4214784 | tf_op jit(solution)/shard_map/while/body/eval_jaxpr/convert_element_type | solution.py:43
  585.7 2.6 fusion.135
  589.6 17.0 %multiply_convert_fusion.19 = (bf16[1024,1024]{1,0:T(8,128)(2,1)S(1)}, bf16[1024,1024]{1,0:T(8,128)(2,1)}) fusion(f32[1024]{0:T(1024)S(1)} %get-tuple-element.234, f32[1024]{0:T(1024)S(1)} %get-tuple-element.235, f32[1024]{0:T(1024)S(1)} %get-tuple-element.236, f32[1024]{0:T(1024)S(1)} %convert_multiply_fusion.2, f32[1024]{0:T(1024)S(1)} %get-tuple-element.237), kind=kLoop, calls=%fused_computation.5.clone.1 | loop fusion | flops 7340032 | bytes 4214784 | tf_op jit(solution)/shard_map/while/body/eval_jaxpr/convert_element_type | solution.py:43
  606.6 2.6 fusion.135
  610.6 17.0 %multiply_convert_fusion.19 = (bf16[1024,1024]{1,0:T(8,128)(2,1)S(1)}, bf16[1024,1024]{1,0:T(8,128)(2,1)}) fusion(f32[1024]{0:T(1024)S(1)} %get-tuple-element.234, f32[1024]{0:T(1024)S(1)} %get-tuple-element.235, f32[1024]{0:T(1024)S(1)} %get-tuple-element.236, f32[1024]{0:T(1024)S(1)} %convert_multiply_fusion.2, f32[1024]{0:T(1024)S(1)} %get-tuple-element.237), kind=kLoop, calls=%fused_computation.5.clone.1 | loop fusion | flops 7340032 | bytes 4214784 | tf_op jit(solution)/shard_map/while/body/eval_jaxpr/convert_element_type | solution.py:43
  627.5 2.6 fusion.135
  631.5 17.0 %multiply_convert_fusion.19 = (bf16[1024,1024]{1,0:T(8,128)(2,1)S(1)}, bf16[1024,1024]{1,0:T(8,128)(2,1)}) fusion(f32[1024]{0:T(1024)S(1)} %get-tuple-element.234, f32[1024]{0:T(1024)S(1)} %get-tuple-element.235, f32[1024]{0:T(1024)S(1)} %get-tuple-element.236, f32[1024]{0:T(1024)S(1)} %convert_multiply_fusion.2, f32[1024]{0:T(1024)S(1)} %get-tuple-element.237), kind=kLoop, calls=%fused_computation.5.clone.1 | loop fusion | flops 7340032 | bytes 4214784 | tf_op jit(solution)/shard_map/while/body/eval_jaxpr/convert_element_type | solution.py:43
  648.4 2.6 fusion.135
  652.4 17.0 %multiply_convert_fusion.19 = (bf16[1024,1024]{1,0:T(8,128)(2,1)S(1)}, bf16[1024,1024]{1,0:T(8,128)(2,1)}) fusion(f32[1024]{0:T(1024)S(1)} %get-tuple-element.234, f32[1024]{0:T(1024)S(1)} %get-tuple-element.235, f32[1024]{0:T(1024)S(1)} %get-tuple-element.236, f32[1024]{0:T(1024)S(1)} %convert_multiply_fusion.2, f32[1024]{0:T(1024)S(1)} %get-tuple-element.237), kind=kLoop, calls=%fused_computation.5.clone.1 | loop fusion | flops 7340032 | bytes 4214784 | tf_op jit(solution)/shard_map/while/body/eval_jaxpr/convert_element_type | solution.py:43
  669.3 2.6 fusion.135
  673.3 17.0 %multiply_convert_fusion.19 = (bf16[1024,1024]{1,0:T(8,128)(2,1)S(1)}, bf16[1024,1024]{1,0:T(8,128)(2,1)}) fusion(f32[1024]{0:T(1024)S(1)} %get-tuple-element.234, f32[1024]{0:T(1024)S(1)} %get-tuple-element.235, f32[1024]{0:T(1024)S(1)} %get-tuple-element.236, f32[1024]{0:T(1024)S(1)} %convert_multiply_fusion.2, f32[1024]{0:T(1024)S(1)} %get-tuple-element.237), kind=kLoop, calls=%fused_computation.5.clone.1 | loop fusion | flops 7340032 | bytes 4214784 | tf_op jit(solution)/shard_map/while/body/eval_jaxpr/convert_element_type | solution.py:43
  690.3 2.6 fusion.135
  694.2 17.0 %multiply_convert_fusion.19 = (bf16[1024,1024]{1,0:T(8,128)(2,1)S(1)}, bf16[1024,1024]{1,0:T(8,128)(2,1)}) fusion(f32[1024]{0:T(1024)S(1)} %get-tuple-element.234, f32[1024]{0:T(1024)S(1)} %get-tuple-element.235, f32[1024]{0:T(1024)S(1)} %get-tuple-element.236, f32[1024]{0:T(1024)S(1)} %convert_multiply_fusion.2, f32[1024]{0:T(1024)S(1)} %get-tuple-element.237), kind=kLoop, calls=%fused_computation.5.clone.1 | loop fusion | flops 7340032 | bytes 4214784 | tf_op jit(solution)/shard_map/while/body/eval_jaxpr/convert_element_type | solution.py:43
  711.2 2.6 fusion.135
  715.1 17.0 %multiply_convert_fusion.19 = (bf16[1024,1024]{1,0:T(8,128)(2,1)S(1)}, bf16[1024,1024]{1,0:T(8,128)(2,1)}) fusion(f32[1024]{0:T(1024)S(1)} %get-tuple-element.234, f32[1024]{0:T(1024)S(1)} %get-tuple-element.235, f32[1024]{0:T(1024)S(1)} %get-tuple-element.236, f32[1024]{0:T(1024)S(1)} %convert_multiply_fusion.2, f32[1024]{0:T(1024)S(1)} %get-tuple-element.237), kind=kLoop, calls=%fused_computation.5.clone.1 | loop fusion | flops 7340032 | bytes 4214784 | tf_op jit(solution)/shard_map/while/body/eval_jaxpr/convert_element_type | solution.py:43
  732.1 2.6 fusion.135
  (124 shorter events, 21.2 us)
Async XLA Ops:
  72.4 63.6 %copy-start.11 = (bf16[2,128,2048]{2,1,0:T(8,128)(2,1)S(1)}, bf16[2,128,2048]{2,1,0:T(8,128)(2,1)}, u32[]{:S(2)}) copy-start(bf16[2,128,2048]{2,1,0:T(8,128)(2,1)} %param.6) | copy-start | bytes 3145732
  144.6 115.6 %all-to-all-start = ((bf16[2,2,1024,128]{3,1,0,2:T(2,128)(2,1)}), bf16[2,2,1024,128]{3,1,0,2:T(2,128)(2,1)S(1)}, u32[]{:S(2)}, u32[]{:S(2)}) async-start(bf16[2,2,1024,128]{3,1,0,2:T(2,128)(2,1)} %pad_maximum_fusion.8), calls=%async_computation | async-start | bytes 2097152 | tf_op jit(solution)/shard_map/all_to_all | solution.py:75
  224.2 51.8 %copy-start.6 = (bf16[1024,1024]{1,0:T(8,128)(2,1)}, bf16[1024,1024]{1,0:T(8,128)(2,1)S(1)}, u32[]{:S(2)}) copy-start(bf16[1024,1024]{1,0:T(8,128)(2,1)S(1)} %get-tuple-element.182) | copy-start | bytes 6291460
  260.1 2.2 copy-start
  262.3 4.3 copy-start.1
  266.7 1.6 copy-start.8
  268.3 2.2 copy-start.3
  269.1 2.8 copy-start.2
  276.8 10.2 %copy-start.10 = (s32[2,1,16]{2,1,0:T(1,128)S(1)}, s32[2,1,16]{2,1,0:T(1,128)}, u32[]{:S(2)}) copy-start(s32[2,1,16]{2,1,0:T(1,128)} %param.8) | copy-start | bytes 388
  279.4 19.7 %all-to-all-start.1 = ((bf16[16,2,8192]{2,1,0:T(2,128)(2,1)}), bf16[16,2,8192]{2,1,0:T(2,128)(2,1)S(1)}, u32[]{:S(2)}, u32[]{:S(2)}) async-start(bf16[16,2,8192]{2,1,0:T(2,128)(2,1)} %reshape.152), calls=%async_computation.1 | async-start | bytes 1048576 | tf_op jit(solution)/shard_map/all_to_all | solution.py:92
  286.8 113.3 %all-gather.2.cloned.1.call-start = ((), (), s32[]{:S(2)}) async-start(), calls=%async_computation.2 | async-start | bytes 4718592 | tf_op jit(solution)/shard_map/all_gather | solution.py:119
  301.2 3.2 copy-start.7
  301.2 3.5 copy-start.9
  304.7 1.6 copy-start.4
  304.7 2.2 copy-start.5
  311.6 88.5 %copy-start.12 = (s32[16]{0:T(128)S(1)}, s32[16]{0:T(128)}, u32[]{:S(2)}) copy-start(s32[16]{0:T(128)} %param.9) | copy-start | bytes 196
  734.7 0.7 copy-start.13
Sparse Core Ops, SparseCore 0:
  314.0 86.0 all-gather.1
where the time goes:
time: 753 us; the launch traced here: 743 us
  other arithmetic  509 us (68%)
  waiting for transfers between devices  98 us (13%)
  matrix products  68.4 us (9%)
  local copies, waits for them, and re-layouts  22.9 us (3%)
  between operations  16.7 us (2%)
  starting transfers between devices  14.9 us (2%)
  loops' own time  12.2 us (2%)
    convert_element_type x16, other arithmetic, plane_kernel(): real_part = (weight[:, None] * jnp.cos(phases)).astype(jnp.bfloat16)  271 us
    convert_element_type x5, other arithmetic, turn_table(): (jnp.cos(angles) * factor).astype(jnp.bfloat16)  170 us
    all_gather x1, waiting for transfers between devices, per_device(): arriving = lax.all_gather(filters, 'angle', axis=0, tiled=True)  86.2 us
    neg x2, other arithmetic, per_device(): stacked = jnp.concatenate([cols_cos, -cols_sin], axis=1)  63.4 us
    dot_general x28, matrix products, mat(): return jnp.dot(left, right, preferred_element_type=jnp.float32)  57.7 us
  transfers between devices with their start and end apart: 3, of which 2 were waited for; matrix products, arithmetic and copies ran while one was open for 14% of the time, Pallas kernels for 0%

commit v1 on v0

v1 whole, which is shorter than its diff:
```python
import functools
import math

import jax
import jax.numpy as jnp
import numpy as np
from jax import lax
from jax.experimental import pallas as pl
from jax.experimental.pallas import tpu as pltpu
from jax.sharding import PartitionSpec as P

PIX = 2048
CROP = 1024
BLOCK = 64
PLANES = 8
ANGLES = 1200
HOLOS = 16

ROWS = 16
GROUPS = 8
HELD = HOLOS // GROUPS
SLAB = CROP // ROWS
LANE = 128
WIDE = 256
SLABS = CROP // LANE

MESH = pl.DeviceIdType.MESH
f32 = jnp.float32
bf16 = jnp.bfloat16

SIN = (6.283185302511503, -41.34170040531721, 81.6051313857832, -76.70301535364747, 42.02592698447418,
       -14.899846663536497, 3.2381375046186873)
COS = (0.9999999890590228, -19.73920449945383, 64.93911745989081, -85.45013953079767, 60.167630950263465,
       -25.967599245923743, 6.52865815775625)
ATAN = (0.9999999842426363, -0.33333066780691484, 0.19992483578502865, -0.14202570511730603, 0.10636754098309847,
        -0.07495445443851168, 0.04258760747298536, -0.016005030509000328, 0.002834064300549813)


def poly(coefs, v):
    total = jnp.full_like(v, coefs[-1])
    for coef in coefs[-2::-1]:
        total = total * v + f32(coef)
    return total


def turns(x):
    u = x - jnp.round(x)
    v = u * u
    return poly(COS, v), u * poly(SIN, v)


def half_band(n):
    n = n.astype(np.float64)
    with np.errstate(all="ignore"):
        odd = np.sin(np.pi * n / 2) / np.sin(np.pi * n / PIX) / CROP
    return np.where(n == 0, 1.0, np.where(n % 2 == 0, 0.0, odd))


def half_band_strips():
    x = np.arange(PIX + 3 * 512)[:, None] - 3 * 512
    b = np.arange(WIDE)
    along_x = half_band(2 * b[None, :] - x)
    i = np.arange(CROP + 3 * WIDE)[None, :] - 3 * WIDE
    along_y = half_band(2 * (b[:, None] - i) - 1)
    return along_x.astype(bf16), along_y.astype(bf16)


def iota(shape, dim):
    return lax.broadcasted_iota(jnp.int32, shape, dim)


def dot(a, b):
    return jnp.dot(a, b, preferred_element_type=f32)


def kernel(centres, angle_index, offsets, hologram, x_hbm, y_hbm, out,
           x_strip, y_strip, q_tab, p_tab, lhs, even, send1, recv1, send2, recv2, rot, ryt, wave, back, plane_tab,
           spread, acc, own, send3, recv3, copy_sem, s1, r1, s2, r2, s3, r3):
    row = lax.axis_index("row")
    group = lax.axis_index("angle")

    x_copy = pltpu.make_async_copy(x_hbm, x_strip, copy_sem.at[0])
    y_copy = pltpu.make_async_copy(y_hbm, y_strip, copy_sem.at[1])
    x_copy.start()
    y_copy.start()

    barrier = pltpu.get_barrier_semaphore()

    def greet_row(i, carry):
        pl.semaphore_signal(barrier, inc=1, device_id={"row": lax.rem(row + i, ROWS)}, device_id_type=MESH)
        return carry

    def greet_group(i, carry):
        pl.semaphore_signal(barrier, inc=1, device_id={"angle": lax.rem(group + i, GROUPS)}, device_id_type=MESH)
        return carry

    lax.fori_loop(1, ROWS, greet_row, 0)
    lax.fori_loop(1, GROUPS, greet_group, 0)

    at_x = LANE * iota((PIX // LANE, LANE), 0) + iota((PIX // LANE, LANE), 1)
    for h in range(HELD):
        m = (at_x * (2 * centres[h, 0] - 1)) & (2 * PIX - 1)
        c, s = turns(m.astype(f32) * f32(1.0 / (2 * PIX)))
        q_tab[2 * h] = c
        q_tab[2 * h + 1] = -s
    at_y = 2 * SLAB * row + 2 * iota((SLAB, LANE), 0)
    for parity in range(2):
        for h in range(HELD):
            m = ((at_y + (1 - parity)) * (2 * centres[h, 1] - 1)) & (2 * PIX - 1)
            c, s = turns(m.astype(f32) * f32(1.0 / (2 * PIX)))
            p_tab[4 * parity + 2 * h] = 0.5 * c
            p_tab[4 * parity + 2 * h + 1] = -0.5 * s

    wanted = iota((2 * SLAB, 2 * SLAB), 0)
    wanted = jnp.where(wanted < SLAB, 2 * wanted + 1, 2 * wanted - 2 * SLAB)
    sort_rows = jnp.where(wanted == iota((2 * SLAB, 2 * SLAB), 1), 1.0, 0.0).astype(bf16)

    def modulate(k, carry):
        at = pl.multiple_of(WIDE * k, WIDE)
        for h in range(HELD):
            sorted_rows = dot(sort_rows, hologram[h, :, pl.ds(at, WIDE)])
            for part in range(2):
                for side in range(2):
                    phase = q_tab[2 * h + part, pl.ds(2 * k + side, 1), :]
                    for parity in range(2):
                        block = sorted_rows[parity * SLAB:(parity + 1) * SLAB, side * LANE:(side + 1) * LANE]
                        first = 4 * SLAB * parity + 2 * SLAB * h + SLAB * part
                        lhs[first:first + SLAB, pl.ds(pl.multiple_of(at + side * LANE, LANE), LANE)] = (
                            block * phase
                        ).astype(bf16)
        return carry

    lax.fori_loop(0, PIX // WIDE, modulate, 0)
    x_copy.wait()

    def across(parity, block):
        weights = x_strip[pl.ds(pl.multiple_of(3 * 512 - 512 * block, 512), PIX), :]
        z = dot(lhs[4 * SLAB * parity:4 * SLAB * (parity + 1), :], weights)
        for h in range(HELD):
            c = p_tab[4 * parity + 2 * h]
            s = p_tab[4 * parity + 2 * h + 1]
            for side in range(2):
                re = z[2 * SLAB * h:2 * SLAB * h + SLAB, side * LANE:(side + 1) * LANE]
                im = z[2 * SLAB * h + SLAB:2 * SLAB * (h + 1), side * LANE:(side + 1) * LANE]
                yield h, side, re * c - im * s, re * s + im * c

    def to_row(send, recv, sends, recvs, to):
        return pltpu.make_async_remote_copy(
            src_ref=send.at[to], dst_ref=recv.at[row], send_sem=sends.at[to], recv_sem=recvs.at[row],
            device_id={"row": to}, device_id_type=MESH)

    def from_row(send, recv, sends, recvs, source):
        return pltpu.make_async_remote_copy(
            src_ref=send.at[source], dst_ref=recv.at[source], send_sem=sends.at[source], recv_sem=recvs.at[source],
            device_id={"row": source}, device_id_type=MESH)

    pl.semaphore_wait(barrier, ROWS + GROUPS - 2)

    def odd_rows(k, carry):
        block = lax.rem(row + k, 4)
        for h, side, re, im in across(0, block):
            to = SLABS * h + 2 * block + side
            send1[to, :, 0:LANE] = re.astype(bf16)
            send1[to, :, LANE:WIDE] = im.astype(bf16)

            @pl.when(to != row)
            def _():
                to_row(send1, recv1, s1, r1, to).start()

            @pl.when(to == row)
            def _():
                recv1[row] = send1[row]
        return carry

    lax.fori_loop(0, 4, odd_rows, 0)

    def even_rows(block, carry):
        for h, side, re, im in across(1, block):
            at = pl.ds(pl.multiple_of(WIDE * block + LANE * side, LANE), LANE)
            even[2 * h, :, at] = re
            even[2 * h + 1, :, at] = im
        return carry

    lax.fori_loop(0, 4, even_rows, 0)

    def table(freq, store):
        chunk = 16
        lanes = iota((chunk, LANE), 1).astype(f32)

        def rows_of(k, carry):
            at = pl.multiple_of(chunk * k, chunk)
            j = (iota((chunk, LANE), 0) + (chunk * k - CROP // 2)).astype(f32)
            alpha = freq(j)
            c0, s0 = turns(alpha * lanes)
            cr, sr = turns(alpha * f32(LANE))
            c, s = c0, s0
            for a in range(4):
                store(at, a + 4, c, -s)
                if a < 3:
                    c, s = c * cr - s * sr, s * cr + c * sr
            c, s = c0, s0
            for a in range(3, -1, -1):
                c, s = c * cr + s * sr, s * cr - c * sr
                store(at, a, c, -s)
            return carry

        lax.fori_loop(0, CROP // chunk, rows_of, 0)

    def wave_store(at, a, c, s):
        wave[pl.ds(at, 16), a * LANE:(a + 1) * LANE] = c.astype(bf16)
        wave[pl.ds(at, 16), CROP + a * LANE:CROP + (a + 1) * LANE] = s.astype(bf16)

    table(lambda j: j * f32(1.0 / CROP), wave_store)

    def tilt(h, shape):
        index = jnp.full(shape, angle_index[HELD * group + h], jnp.int32)
        return turns(index.astype(f32) * f32(1.0 / ANGLES))

    def axial(spatial):
        turn = spatial * f32(2.0 * math.pi)
        return (jnp.sqrt(16.0 - turn * turn) - 4.0) * f32(0.5 / math.pi)

    def back_table(h):
        c, s = tilt(h, (16, LANE))

        def freq(j):
            spatial = j * f32(1.0 / CROP)
            return spatial * c - axial(spatial) * s

        def store(at, a, c, s):
            back[pl.ds(2 * h * CROP + at, 16), a * LANE:(a + 1) * LANE] = c.astype(bf16)
            back[pl.ds((2 * h + 1) * CROP + at, 16), a * LANE:(a + 1) * LANE] = s.astype(bf16)

        table(freq, store)

    back_table(0)

    y_copy.wait()

    def wait_first(i, carry):
        from_row(send1, recv1, s1, r1, lax.rem(row + i, ROWS)).wait_recv()
        return carry

    lax.fori_loop(1, ROWS, wait_first, 0)
    gathered = recv1[...].reshape(CROP, WIDE)

    def down(k, carry):
        block = lax.rem(row // 4 + k, 4)
        weights = y_strip[:, pl.ds(pl.multiple_of(3 * WIDE - WIDE * block, WIDE), CROP)]
        z = dot(weights, gathered).astype(bf16)
        for part in range(4):
            to = 4 * block + part
            send2[to] = z[SLAB * part:SLAB * (part + 1), :]

            @pl.when(to != row)
            def _():
                to_row(send2, recv2, s2, r2, to).start()

            @pl.when(to == row)
            def _():
                recv2[row] = send2[row]
        return carry

    lax.fori_loop(0, 4, down, 0)

    back_table(1)

    spatial = (LANE * iota((SLABS, LANE), 0) + iota((SLABS, LANE), 1) - CROP // 2).astype(f32) * f32(1.0 / CROP)
    ramp = jnp.abs(spatial) * f32(2.0 / math.sqrt(CROP * HOLOS) / math.sqrt(CROP))
    for h in range(HELD):
        c, s = tilt(h, (SLABS, LANE))
        beta = spatial * s + axial(spatial) * c
        for d in range(PLANES):
            pc, ps = turns(beta * f32(d - PLANES // 2))
            plane_tab[2 * (PLANES * h + d)] = pc * ramp
            plane_tab[2 * (PLANES * h + d) + 1] = ps * ramp

    def rotations(k, carry):
        at = LANE * k
        m = (iota((SLAB, LANE), 1) + at + iota((SLAB, LANE), 0) + SLAB * row).astype(f32)
        c, s = turns(m * f32(0.5 / CROP))
        lanes = pl.ds(pl.multiple_of(at, LANE), LANE)
        rot[0, :, lanes] = c
        rot[1, :, lanes] = -s
        return carry

    lax.fori_loop(0, SLABS, rotations, 0)

    left_half = iota((SLAB, LANE), 1) < BLOCK

    def rytov(i, carry):
        source = lax.rem(row + i, ROWS)

        @pl.when(i > 0)
        def _():
            from_row(send2, recv2, s2, r2, source).wait_recv()

        h = source // SLABS
        slab = lax.rem(source, SLABS)
        lanes = pl.ds(pl.multiple_of(LANE * slab, LANE), LANE)
        re = even[2 * h, :, lanes] + recv2[source, :, 0:LANE].astype(f32)
        im = even[2 * h + 1, :, lanes] + recv2[source, :, LANE:WIDE].astype(f32)
        c = rot[0, :, lanes]
        s = rot[1, :, lanes]
        field_re = re * c - im * s
        field_im = re * s + im * c
        energy = field_re * field_re + field_im * field_im + 1.0
        t = field_im / (jnp.sqrt(energy) + jnp.abs(field_re))
        unwrap = jnp.where(left_half, offsets[h, 0, 2 * slab], offsets[h, 0, 2 * slab + 1]).astype(f32)
        turned = 2.0 * (t * poly(ATAN, t * t)) + f32(2.0 * math.pi) * unwrap
        at = pl.multiple_of(2 * SLAB * h, 2 * SLAB)
        ryt[pl.ds(at, SLAB), lanes] = (0.5 * jnp.log(energy)).astype(bf16)
        ryt[pl.ds(pl.multiple_of(at + SLAB, SLAB), SLAB), lanes] = turned.astype(bf16)
        return carry

    lax.fori_loop(0, ROWS, rytov, 0)

    def filtered(k, carry):
        at = pl.multiple_of(WIDE * k, WIDE)
        fc = dot(ryt[...], wave[:, pl.ds(at, WIDE)])
        fs = dot(ryt[...], wave[:, pl.ds(pl.multiple_of(CROP + at, WIDE), WIDE)])
        for h in range(HELD):
            top = slice(2 * SLAB * h, 2 * SLAB * h + SLAB)
            low = slice(2 * SLAB * h + SLAB, 2 * SLAB * (h + 1))
            re = fc[top] - fs[low]
            im = fc[low] + fs[top]
            for side in range(2):
                lanes = slice(side * LANE, (side + 1) * LANE)
                re_side, im_side = re[:, lanes], im[:, lanes]
                real_at = pl.ds(pl.multiple_of(2 * CROP * h + at + side * LANE, LANE), LANE)
                imag_at = pl.ds(pl.multiple_of(2 * CROP * h + CROP + at + side * LANE, LANE), LANE)
                for d in range(PLANES):
                    pc = plane_tab[2 * (PLANES * h + d), pl.ds(2 * k + side, 1), :]
                    ps = plane_tab[2 * (PLANES * h + d) + 1, pl.ds(2 * k + side, 1), :]
                    spread[d * SLAB:(d + 1) * SLAB, real_at] = (re_side * pc - im_side * ps).astype(bf16)
                    spread[d * SLAB:(d + 1) * SLAB, imag_at] = (re_side * ps + im_side * pc).astype(bf16)
        return carry

    lax.fori_loop(0, CROP // WIDE, filtered, 0)

    def to_group(k, to):
        return pltpu.make_async_remote_copy(
            src_ref=send3.at[k, to], dst_ref=recv3.at[k, group], send_sem=s3.at[k, to], recv_sem=r3.at[k, group],
            device_id={"angle": to}, device_id_type=MESH)

    def from_group(k, source):
        return pltpu.make_async_remote_copy(
            src_ref=send3.at[k, source], dst_ref=recv3.at[k, source], send_sem=s3.at[k, source],
            recv_sem=r3.at[k, source], device_id={"angle": source}, device_id_type=MESH)

    def planes(k, carry):
        at = pl.multiple_of(WIDE * k, WIDE)
        acc[...] = dot(spread[...], back[:, pl.ds(at, WIDE)])
        own[:, pl.ds(at, WIDE)] = acc[pl.ds(pl.multiple_of(SLAB * group, SLAB), SLAB), :]
        for d in range(PLANES):
            send3[k, d] = acc[d * SLAB:(d + 1) * SLAB, :].astype(bf16)

        def push(j, carry):
            to_group(k, lax.rem(group + j, GROUPS)).start()
            return carry

        lax.fori_loop(1, GROUPS, push, 0)
        return carry

    lax.fori_loop(0, CROP // WIDE, planes, 0)

    def collect(k, carry):
        at = pl.multiple_of(WIDE * k, WIDE)

        def take(j, total):
            source = lax.rem(group + j, GROUPS)
            from_group(k, source).wait_recv()
            return total + recv3[k, source].astype(f32)

        out[0, :, pl.ds(at, WIDE)] = lax.fori_loop(1, GROUPS, take, own[:, pl.ds(at, WIDE)])
        return carry

    lax.fori_loop(0, CROP // WIDE, collect, 0)

    def sent_row(i, carry):
        to = lax.rem(row + i, ROWS)
        to_row(send1, recv1, s1, r1, to).wait_send()
        to_row(send2, recv2, s2, r2, to).wait_send()
        return carry

    lax.fori_loop(1, ROWS, sent_row, 0)

    def sent_group(i, carry):
        to = lax.rem(group + lax.rem(i, GROUPS - 1) + 1, GROUPS)
        to_group(i // (GROUPS - 1), to).wait_send()
        return carry

    lax.fori_loop(0, (GROUPS - 1) * (CROP // WIDE), sent_group, 0)


def per_device(x_strip, y_strip, hologram, centres, offsets, angle_index):
    smem = pl.BlockSpec(memory_space=pltpu.SMEM)
    vmem = pl.BlockSpec(memory_space=pltpu.VMEM)
    anywhere = pl.BlockSpec(memory_space=pl.ANY)
    tiles = CROP // WIDE
    return pl.pallas_call(
        kernel,
        out_shape=jax.ShapeDtypeStruct((1, SLAB, CROP), f32),
        in_specs=[smem, smem, smem, vmem, anywhere, anywhere],
        out_specs=vmem,
        scratch_shapes=[
            pltpu.VMEM(x_strip.shape, bf16),
            pltpu.VMEM(y_strip.shape, bf16),
            pltpu.VMEM((2 * HELD, PIX // LANE, LANE), f32),
            pltpu.VMEM((4 * HELD, SLAB, LANE), f32),
            pltpu.VMEM((4 * HELD * SLAB, PIX), bf16),
            pltpu.VMEM((2 * HELD, SLAB, CROP), f32),
            pltpu.VMEM((ROWS, SLAB, WIDE), bf16),
            pltpu.VMEM((ROWS, SLAB, WIDE), bf16),
            pltpu.VMEM((ROWS, SLAB, WIDE), bf16),
            pltpu.VMEM((ROWS, SLAB, WIDE), bf16),
            pltpu.VMEM((2, SLAB, CROP), f32),
            pltpu.VMEM((2 * HELD * SLAB, CROP), bf16),
            pltpu.VMEM((CROP, 2 * CROP), bf16),
            pltpu.VMEM((2 * HELD * CROP, CROP), bf16),
            pltpu.VMEM((2 * HELD * PLANES, SLABS, LANE), f32),
            pltpu.VMEM((PLANES * SLAB, 2 * HELD * CROP), bf16),
            pltpu.VMEM((PLANES * SLAB, WIDE), f32),
            pltpu.VMEM((SLAB, CROP), f32),
            pltpu.VMEM((tiles, GROUPS, SLAB, WIDE), bf16),
            pltpu.VMEM((tiles, GROUPS, SLAB, WIDE), bf16),
            pltpu.SemaphoreType.DMA((2,)),
            pltpu.SemaphoreType.DMA((ROWS,)),
            pltpu.SemaphoreType.DMA((ROWS,)),
            pltpu.SemaphoreType.DMA((ROWS,)),
            pltpu.SemaphoreType.DMA((ROWS,)),
            pltpu.SemaphoreType.DMA((tiles, GROUPS)),
            pltpu.SemaphoreType.DMA((tiles, GROUPS)),
        ],
        compiler_params=pltpu.CompilerParams(
            collective_id=0, has_side_effects=True, vmem_limit_bytes=56 * 1024 * 1024
        ),
    )(centres, angle_index, offsets, hologram, x_strip, y_strip)


def solution(mesh):
    x_strip, y_strip = half_band_strips()
    placed = (P("angle", "row", None), P("angle", None), P("angle", "row", None), P())
    return jax.shard_map(
        functools.partial(per_device, x_strip, y_strip),
        mesh=mesh, in_specs=placed, out_specs=P("angle", "row", None), check_vma=False
    )
```

time: 753 us -> 52.8 us (0.07); the launches traced: 743 us -> 52.5 us
  other arithmetic: 509 us -> 0 us
  waiting for transfers between devices: 98 us -> 0 us
  matrix products: 68.4 us -> 0 us
  Pallas kernels: 0 us -> 50.8 us
  local copies, waits for them, and re-layouts: 22.9 us -> 1.67 us
  between operations: 16.7 us -> 0.01 us
  starting transfers between devices: 14.9 us -> 0 us
  loops' own time: 12.2 us -> 0 us
    convert_element_type x23 -> x0, other arithmetic: 442 us -> none  [the longest x16 271 us: plane_kernel(): real_part = (weight[:, None] * jnp.cos(phases)).astype(jnp.bfloat16)]
    all_gather x1 -> x0, waiting for transfers between devices: 86.2 us -> none  [per_device(): arriving = lax.all_gather(filters, 'angle', axis=0, tiled=True)]
    dot_general x34 -> x0, matrix products: 68.4 us -> none  [the longest x28 57.7 us: mat(): return jnp.dot(left, right, preferred_element_type=jnp.float32)]
    neg x4 -> x0, other arithmetic: 63.5 us -> none  [the longest x2 63.4 us: per_device(): stacked = jnp.concatenate([cols_cos, -cols_sin], axis=1)]
    pallas_call x0 -> x1, Pallas kernels: none -> 50.8 us  [per_device(): pl.pallas_call(kernel, out_shape=jax.ShapeDtypeStruct((1, SLAB, CROP), f3...]
    all_to_all x2 -> x0, starting transfers between devices: 14.6 us -> none  [the longest x1 7.32 us: per_device(): lax.all_to_all(outgoing, 'row', split_axis=2, concat_axis=3, tiled=True)]
    another operation x1 -> x0, loops' own time: 12.2 us -> none  [per_device(): return lax.fori_loop(0, arriving.shape[0], add_one, empty_sum)]
    all_to_all x2 -> x0, waiting for transfers between devices: 11.8 us -> none  [the longest x1 11.8 us: per_device(): lax.all_to_all(middle, 'row', split_axis=3, concat_axis=2, tiled=True)]
  transfers between devices with their start and end apart: 3 -> 0, of which waited for: 2 -> 0; matrix products, arithmetic and copies ran while one was open for 14% -> 0% of each run, Pallas kernels for 0% -> 0%
where the time goes in v1:
time: 52.8 us; the launch traced here: 52.5 us
  Pallas kernels  50.8 us (96%)
  local copies, waits for them, and re-layouts  1.67 us (3%)
    pallas_call x1, Pallas kernels, per_device(): pl.pallas_call(kernel, out_shape=jax.ShapeDtypeStruct((1, SLAB, CROP), f3...  50.8 us
    unnamed x1, local copies, waits for them, and re-layouts  1.67 us

profile of v1, /device:TPU:8, one launch (start us, length us, event | category | flops | bytes accessed | tf_op | source)
XLA Modules:
  0.0 52.5 jit_solution(12770072546323172888)
XLA Ops:
  0.0 50.8 %shard_map.64 = f32[1,64,1024]{2,1,0:T(8,128)} custom-call(s32[2,2]{1,0:T(2,128)} %centres.1, s32[16]{0:T(128)} %angle_index.1, s32[2,1,16]{2,1,0:T(1,128)} %offsets.1, bf16[2,128,2048]{2,1,0:T(8,128)(2,1)} %hologram.1, bf16[3584,256]{1,0:T(8,128)(2,1)} %constant.4.clone.x_hbm, bf16[256,1792]{1,0:T(8,128)(2,1)} %constant.5.clone.y_hbm), custom_call_target="tpu_custom_call" | custom-call | tf_op jit(solution)/shard_map/pallas_call | solution.py:401
  50.8 1.7 %copy.8 = f32[1,64,1024]{2,1,0:T(8,128)} copy(f32[1,64,1024]{2,1,0:T(8,128)} %shard_map.64) | data formatting | bytes 524288

commit v2 on v1

v2 whole, which is shorter than its diff:
```python
import functools
import math

import jax
import jax.numpy as jnp
import numpy as np
from jax import lax
from jax.experimental import pallas as pl
from jax.experimental.pallas import tpu as pltpu
from jax.sharding import PartitionSpec as P

PIX = 2048
CROP = 1024
BLOCK = 64
PLANES = 8
ANGLES = 1200
HOLOS = 16

ROWS = 16
GROUPS = 8
HELD = HOLOS // GROUPS
SLAB = CROP // ROWS
LANE = 128
WIDE = 256
SLABS = CROP // LANE
HALVES = 2
HALF = SLAB // HALVES
TILE = 512
TILES = CROP // TILE

MESH = pl.DeviceIdType.MESH
f32 = jnp.float32
bf16 = jnp.bfloat16

SIN = (6.283185302511503, -41.34170040531721, 81.6051313857832, -76.70301535364747, 42.02592698447418,
       -14.899846663536497, 3.2381375046186873)
COS = (0.9999999890590228, -19.73920449945383, 64.93911745989081, -85.45013953079767, 60.167630950263465,
       -25.967599245923743, 6.52865815775625)
ATAN = (0.9999999842426363, -0.33333066780691484, 0.19992483578502865, -0.14202570511730603, 0.10636754098309847,
        -0.07495445443851168, 0.04258760747298536, -0.016005030509000328, 0.002834064300549813)


def poly(coefs, v):
    total = jnp.full_like(v, coefs[-1])
    for coef in coefs[-2::-1]:
        total = total * v + f32(coef)
    return total


def turns(x):
    u = x - jnp.round(x)
    v = u * u
    return poly(COS, v), u * poly(SIN, v)


def half_band(n):
    n = n.astype(np.float64)
    with np.errstate(all="ignore"):
        odd = np.sin(np.pi * n / 2) / np.sin(np.pi * n / PIX) / CROP
    return np.where(n == 0, 1.0, np.where(n % 2 == 0, 0.0, odd))


def half_band_strips():
    x = np.arange(PIX + 3 * 512)[:, None] - 3 * 512
    b = np.arange(WIDE)
    along_x = half_band(2 * b[None, :] - x)
    i = np.arange(CROP + 3 * WIDE)[None, :] - 3 * WIDE
    b = b.reshape(4, HALVES, HALF).transpose(1, 0, 2).reshape(WIDE)
    along_y = half_band(2 * (b[:, None] - i) - 1)
    return along_x.astype(bf16), along_y.astype(bf16)


def iota(shape, dim):
    return lax.broadcasted_iota(jnp.int32, shape, dim)


def dot(a, b):
    return jnp.dot(a, b, preferred_element_type=f32)


def dot_t(a, b):
    return lax.dot_general(a, b, (((1,), (1,)), ((), ())), preferred_element_type=f32)


def kernel(centres, angle_index, offsets, hologram, x_hbm, y_hbm, out,
           x_strip, y_strip, raw, q_tab, p_tab, odd, evens, even, send1, recv1, send2, recv2, rot, ryt, wave, back,
           turn_tab, plane_tab, spread, own, send3, recv3, copy_sem, s1, r1, s2, r2, s3, r3):
    row = lax.axis_index("row")
    group = lax.axis_index("angle")

    x_copy = pltpu.make_async_copy(x_hbm, x_strip, copy_sem.at[0])
    y_copy = pltpu.make_async_copy(y_hbm, y_strip, copy_sem.at[1])
    x_copy.start()
    y_copy.start()

    barrier = pltpu.get_barrier_semaphore()

    def greet_row(i, carry):
        pl.semaphore_signal(barrier, inc=1, device_id={"row": lax.rem(row + i, ROWS)}, device_id_type=MESH)
        return carry

    def greet_group(i, carry):
        pl.semaphore_signal(barrier, inc=1, device_id={"angle": lax.rem(group + i, GROUPS)}, device_id_type=MESH)
        return carry

    lax.fori_loop(1, ROWS, greet_row, 0)
    lax.fori_loop(1, GROUPS, greet_group, 0)

    at_x = LANE * iota((PIX // LANE, LANE), 0) + iota((PIX // LANE, LANE), 1)
    for h in range(HELD):
        m = (at_x * (2 * centres[h, 0] - 1)) & (2 * PIX - 1)
        c, s = turns(m.astype(f32) * f32(1.0 / (2 * PIX)))
        q_tab[2 * h] = c
        q_tab[2 * h + 1] = -s
    at_y = 2 * SLAB * row + 2 * iota((SLAB, LANE), 0)

    def row_phases(parity):
        for h in range(HELD):
            m = ((at_y + (1 - parity)) * (2 * centres[h, 1] - 1)) & (2 * PIX - 1)
            c, s = turns(m.astype(f32) * f32(1.0 / (2 * PIX)))
            p_tab[2 * h] = 0.5 * c
            p_tab[2 * h + 1] = -0.5 * s

    def modulate(parity, to):
        for a in range(PIX // LANE):
            lanes = slice(a * LANE, (a + 1) * LANE)
            for h in range(HELD):
                if parity == 0:
                    raw[h, a] = hologram[h, :, lanes].astype(f32)
                block = raw[h, a, pl.ds(1 - parity, SLAB, stride=2), :]
                for part in range(2):
                    first = 2 * SLAB * h + SLAB * part
                    to[first:first + SLAB, lanes] = (block * q_tab[2 * h + part, a:a + 1, :]).astype(bf16)

    def across(source, block):
        weights = x_strip[pl.ds(pl.multiple_of(3 * 512 - 512 * block, 512), PIX), :]
        z = dot(source[...], weights)
        for h in range(HELD):
            for side in range(2):
                c = p_tab[2 * h]
                s = p_tab[2 * h + 1]
                re = z[2 * SLAB * h:2 * SLAB * h + SLAB, side * LANE:(side + 1) * LANE]
                im = z[2 * SLAB * h + SLAB:2 * SLAB * (h + 1), side * LANE:(side + 1) * LANE]
                yield h, side, re * c - im * s, re * s + im * c

    modulate(0, odd)
    row_phases(0)
    x_copy.wait()
    pl.semaphore_wait(barrier, ROWS + GROUPS - 2)

    def first_copy(to):
        return pltpu.make_async_remote_copy(
            src_ref=send1.at[to], dst_ref=recv1.at[row], send_sem=s1.at[0], recv_sem=r1.at[0],
            device_id={"row": to}, device_id_type=MESH)

    def odd_rows(k, carry):
        pair = lax.rem(row // 4 + k, 2)
        for half in range(2):
            block = 2 * pair + half
            for h, side, re, im in across(odd, block):
                to = SLABS * h + 2 * block + side
                send1[to, :, 0:LANE] = re.astype(bf16)
                send1[to, :, LANE:WIDE] = im.astype(bf16)

        def push(i, carry):
            to = SLABS * (i // 4) + 4 * pair + lax.rem(row + i, 4)

            @pl.when(to != row)
            def _():
                first_copy(to).start()

            @pl.when(to == row)
            def _():
                recv1[row] = send1[row]
            return carry

        lax.fori_loop(0, 8, push, 0)
        return carry

    lax.fori_loop(0, 2, odd_rows, 0)

    def even_rows():
        modulate(1, evens)
        row_phases(1)
        for block in range(4):
            for h, side, re, im in across(evens, block):
                lanes = slice(WIDE * block + LANE * side, WIDE * block + LANE * (side + 1))
                even[2 * h, :, lanes] = re
                even[2 * h + 1, :, lanes] = im

    even_rows()

    def table(freq, target, cos_at):
        step = 16
        fine = iota((step, LANE), 0).astype(f32)
        coarse = ((iota((CROP // step, LANE), 0) - CROP // step // 2) * step).astype(f32)

        def columns(k, carry):
            def along(shape):
                return freq((iota(shape, 1) + (LANE * k - CROP // 2)).astype(f32))

            c0, s0 = turns(along((step, LANE)) * fine)
            c1, s1 = turns(along((CROP // step, LANE)) * coarse)
            turn_tab[0] = c1
            turn_tab[1] = s1
            cos_lanes = pl.ds(pl.multiple_of(cos_at + LANE * k, LANE), LANE)
            sin_lanes = pl.ds(pl.multiple_of(cos_at + CROP + LANE * k, LANE), LANE)
            for a in range(CROP // step):
                c = turn_tab[0, a:a + 1, :]
                s = turn_tab[1, a:a + 1, :]
                target[a * step:(a + 1) * step, cos_lanes] = (c0 * c - s0 * s).astype(bf16)
                target[a * step:(a + 1) * step, sin_lanes] = -(s0 * c + c0 * s).astype(bf16)
            return carry

        lax.fori_loop(0, SLABS, columns, 0)

    def tilt(h, shape):
        index = jnp.full(shape, angle_index[HELD * group + h], jnp.int32)
        return turns(index.astype(f32) * f32(1.0 / ANGLES))

    def axial(spatial):
        turn = spatial * f32(2.0 * math.pi)
        return (jnp.sqrt(16.0 - turn * turn) - 4.0) * f32(0.5 / math.pi)

    def back_table(h):
        def freq(j):
            c, s = tilt(h, j.shape)
            spatial = j * f32(1.0 / CROP)
            return spatial * c - axial(spatial) * s

        table(freq, back, 2 * h * CROP)

    table(lambda j: j * f32(1.0 / CROP), wave, 0)

    y_copy.wait()
    pltpu.make_async_remote_copy(
        src_ref=send1.at[0:ROWS - 1], dst_ref=recv1.at[0:ROWS - 1], send_sem=s1.at[0], recv_sem=r1.at[0],
        device_id={"row": row}, device_id_type=MESH).wait_recv()

    def second_copy(half, to):
        return pltpu.make_async_remote_copy(
            src_ref=send2.at[half, to], dst_ref=recv2.at[half, row], send_sem=s2.at[half], recv_sem=r2.at[half],
            device_id={"row": to}, device_id_type=MESH)

    def second_all(half):
        return pltpu.make_async_remote_copy(
            src_ref=send2.at[half, 0:ROWS - 1], dst_ref=recv2.at[half, 0:ROWS - 1], send_sem=s2.at[half],
            recv_sem=r2.at[half], device_id={"row": row}, device_id_type=MESH)

    gathered = recv1[...].reshape(CROP, WIDE)
    for half in range(HALVES):
        for block in range(4):
            first = 3 * WIDE - WIDE * block
            z = dot(y_strip[half * 4 * HALF:(half + 1) * 4 * HALF, first:first + CROP], gathered).astype(bf16)
            for part in range(4):
                send2[half, 4 * block + part] = z[HALF * part:HALF * (part + 1), :]

        def push(i, carry):
            second_copy(half, lax.rem(row + i, ROWS)).start()
            return carry

        lax.fori_loop(1, ROWS, push, 0)
        recv2[half, row] = send2[half, row]

    back_table(0)
    back_table(1)

    spatial = (LANE * iota((SLABS, LANE), 0) + iota((SLABS, LANE), 1) - CROP // 2).astype(f32) * f32(1.0 / CROP)
    ramp = jnp.abs(spatial) * f32(2.0 / math.sqrt(CROP * HOLOS) / math.sqrt(CROP))
    for h in range(HELD):
        c, s = tilt(h, (SLABS, LANE))
        beta = spatial * s + axial(spatial) * c
        for z in range(PLANES // 2 + 1):
            pc, ps = turns(beta * f32(z))
            plane_tab[h, z, 0] = pc * ramp
            plane_tab[h, z, 1] = ps * ramp

    def rotations(k, carry):
        at = LANE * k
        m = (iota((SLAB, LANE), 1) + at + iota((SLAB, LANE), 0) + SLAB * row).astype(f32)
        c, s = turns(m * f32(0.5 / CROP))
        lanes = pl.ds(pl.multiple_of(at, LANE), LANE)
        rot[0, :, lanes] = c
        rot[1, :, lanes] = -s
        return carry

    lax.fori_loop(0, SLABS, rotations, 0)

    left_half = iota((HALF, LANE), 1) < BLOCK

    def rytov(half):
        rows = slice(half * HALF, (half + 1) * HALF)

        def slab_of(slab, carry):
            lanes = pl.ds(pl.multiple_of(LANE * slab, LANE), LANE)
            c = rot[0, rows, lanes]
            s = rot[1, rows, lanes]
            for h in range(HELD):
                re = even[2 * h, rows, lanes] + recv2[half, SLABS * h + slab, :, 0:LANE].astype(f32)
                im = even[2 * h + 1, rows, lanes] + recv2[half, SLABS * h + slab, :, LANE:WIDE].astype(f32)
                field_re = re * c - im * s
                field_im = re * s + im * c
                energy = field_re * field_re + field_im * field_im + 1.0
                t = field_im / (jnp.sqrt(energy) + jnp.abs(field_re))
                unwrap = jnp.where(left_half, offsets[h, 0, 2 * slab], offsets[h, 0, 2 * slab + 1]).astype(f32)
                turned = 2.0 * (t * poly(ATAN, t * t)) + f32(2.0 * math.pi) * unwrap
                at = 2 * HALF * h
                ryt[half, at:at + HALF, lanes] = (0.5 * jnp.log(energy)).astype(bf16)
                ryt[half, at + HALF:at + 2 * HALF, lanes] = turned.astype(bf16)
            return carry

        lax.fori_loop(0, SLABS, slab_of, 0)

    def filtered(half):
        for k in range(CROP // WIDE):
            at = WIDE * k
            fc = dot(ryt[half], wave[:, at:at + WIDE])
            fs = dot(ryt[half], wave[:, CROP + at:CROP + at + WIDE])
            for h in range(HELD):
                top = slice(2 * HALF * h, 2 * HALF * h + HALF)
                low = slice(2 * HALF * h + HALF, 2 * HALF * (h + 1))
                for side in range(2):
                    lanes = slice(side * LANE, (side + 1) * LANE)
                    re = fc[top, lanes] - fs[low, lanes]
                    im = fc[low, lanes] + fs[top, lanes]
                    cos_at = 2 * CROP * h + at + side * LANE
                    sin_at = cos_at + CROP

                    def put(d, real, imag):
                        spread[half, d * HALF:(d + 1) * HALF, cos_at:cos_at + LANE] = real.astype(bf16)
                        spread[half, d * HALF:(d + 1) * HALF, sin_at:sin_at + LANE] = imag.astype(bf16)

                    mid = PLANES // 2
                    for z in range(mid + 1):
                        pc = plane_tab[h, z, 0, 2 * k + side:2 * k + side + 1, :]
                        ps = plane_tab[h, z, 1, 2 * k + side:2 * k + side + 1, :]
                        re_c, im_c = re * pc, im * pc
                        if z == 0:
                            put(mid, re_c, im_c)
                            continue
                        re_s, im_s = re * ps, im * ps
                        put(mid - z, re_c + im_s, im_c - re_s)
                        if z < mid:
                            put(mid + z, re_c - im_s, im_c + re_s)

    def third_copy(at, j):
        to = lax.rem(group + j, GROUPS)
        return pltpu.make_async_remote_copy(
            src_ref=send3.at[GROUPS * at + to], dst_ref=recv3.at[(GROUPS - 1) * at + j - 1], send_sem=s3.at[0],
            recv_sem=r3.at[at], device_id={"angle": to}, device_id_type=MESH)

    def planes(half):
        for tile in range(TILES):
            at = TILES * half + tile
            lanes = slice(TILE * tile, TILE * (tile + 1))
            z = dot_t(spread[half], back[lanes, :])
            own[...] = z
            for d in range(PLANES):
                send3[GROUPS * at + d] = z[d * HALF:(d + 1) * HALF, :].astype(bf16)

            def push(j, carry):
                third_copy(at, j).start()
                return carry

            lax.fori_loop(1, GROUPS, push, 0)
            out[0, half * HALF:(half + 1) * HALF, lanes] = own[pl.ds(pl.multiple_of(HALF * group, HALF), HALF), :]

    for half in range(HALVES):
        second_all(half).wait_recv()
        rytov(half)
        filtered(half)
        planes(half)

    for at in range(HALVES * TILES):
        first = (GROUPS - 1) * at
        pltpu.make_async_remote_copy(
            src_ref=send3.at[0:GROUPS - 1], dst_ref=recv3.at[first:first + GROUPS - 1], send_sem=s3.at[0],
            recv_sem=r3.at[at], device_id={"angle": group}, device_id_type=MESH).wait_recv()
        rows = slice(at // TILES * HALF, (at // TILES + 1) * HALF)
        lanes = slice(at % TILES * TILE, (at % TILES + 1) * TILE)
        total = out[0, rows, lanes]
        for j in range(GROUPS - 1):
            total = total + recv3[first + j].astype(f32)
        out[0, rows, lanes] = total

    first_all = pltpu.make_async_remote_copy(
        src_ref=send1.at[0:ROWS - 1], dst_ref=recv1.at[0:ROWS - 1], send_sem=s1.at[0], recv_sem=r1.at[0],
        device_id={"row": row}, device_id_type=MESH)
    first_all.wait_send()
    for half in range(HALVES):
        second_all(half).wait_send()
    count = HALVES * TILES * (GROUPS - 1)
    pltpu.make_async_remote_copy(
        src_ref=send3.at[0:count], dst_ref=recv3.at[0:count], send_sem=s3.at[0], recv_sem=r3.at[0],
        device_id={"angle": group}, device_id_type=MESH).wait_send()


def per_device(x_strip, y_strip, hologram, centres, offsets, angle_index):
    smem = pl.BlockSpec(memory_space=pltpu.SMEM)
    vmem = pl.BlockSpec(memory_space=pltpu.VMEM)
    anywhere = pl.BlockSpec(memory_space=pl.ANY)
    return pl.pallas_call(
        kernel,
        out_shape=pltpu.VMEM((1, SLAB, CROP), f32),
        in_specs=[smem, smem, smem, vmem, anywhere, anywhere],
        out_specs=vmem,
        scratch_shapes=[
            pltpu.VMEM(x_strip.shape, bf16),
            pltpu.VMEM(y_strip.shape, bf16),
            pltpu.VMEM((HELD, PIX // LANE, 2 * SLAB, LANE), f32),
            pltpu.VMEM((2 * HELD, PIX // LANE, LANE), f32),
            pltpu.VMEM((2 * HELD, SLAB, LANE), f32),
            pltpu.VMEM((2 * HELD * SLAB, PIX), bf16),
            pltpu.VMEM((2 * HELD * SLAB, PIX), bf16),
            pltpu.VMEM((2 * HELD, SLAB, CROP), f32),
            pltpu.VMEM((ROWS, SLAB, WIDE), bf16),
            pltpu.VMEM((ROWS, SLAB, WIDE), bf16),
            pltpu.VMEM((HALVES, ROWS, HALF, WIDE), bf16),
            pltpu.VMEM((HALVES, ROWS, HALF, WIDE), bf16),
            pltpu.VMEM((2, SLAB, CROP), f32),
            pltpu.VMEM((HALVES, 2 * HELD * HALF, CROP), bf16),
            pltpu.VMEM((CROP, 2 * CROP), bf16),
            pltpu.VMEM((CROP, 2 * HELD * CROP), bf16),
            pltpu.VMEM((2, CROP // 16, LANE), f32),
            pltpu.VMEM((HELD, PLANES // 2 + 1, 2, SLABS, LANE), f32),
            pltpu.VMEM((HALVES, PLANES * HALF, 2 * HELD * CROP), bf16),
            pltpu.VMEM((PLANES * HALF, TILE), f32),
            pltpu.VMEM((HALVES * TILES * GROUPS, HALF, TILE), bf16),
            pltpu.VMEM((HALVES * TILES * (GROUPS - 1), HALF, TILE), bf16),
            pltpu.SemaphoreType.DMA((2,)),
            pltpu.SemaphoreType.DMA((1,)),
            pltpu.SemaphoreType.DMA((1,)),
            pltpu.SemaphoreType.DMA((HALVES,)),
            pltpu.SemaphoreType.DMA((HALVES,)),
            pltpu.SemaphoreType.DMA((1,)),
            pltpu.SemaphoreType.DMA((HALVES * TILES,)),
        ],
        compiler_params=pltpu.CompilerParams(
            collective_id=0, has_side_effects=True, vmem_limit_bytes=56 * 1024 * 1024
        ),
    )(centres, angle_index, offsets, hologram, x_strip, y_strip)


def solution(mesh):
    x_strip, y_strip = half_band_strips()
    placed = (P("angle", "row", None), P("angle", None), P("angle", "row", None), P())
    return jax.shard_map(
        functools.partial(per_device, x_strip, y_strip),
        mesh=mesh, in_specs=placed, out_specs=P("angle", "row", None), check_vma=False
    )
```

time: 52.8 us -> 42.4 us (0.80)
  Pallas kernels: 50.8 us -> 41.5 us
  local copies, waits for them, and re-layouts: 1.67 us -> 0.71 us
    pallas_call x1, Pallas kernels: 50.8 us -> 41.5 us  [per_device(): pl.pallas_call(kernel, out_shape=pltpu.VMEM((1, SLAB, CROP), f32), in_spe...]
    unnamed x1, local copies, waits for them, and re-layouts: 1.67 us -> 0.71 us
where the time goes in v2:
time: 42.4 us; the launch traced here: 42.2 us
  Pallas kernels  41.5 us (98%)
  local copies, waits for them, and re-layouts  0.71 us (2%)
    pallas_call x1, Pallas kernels, per_device(): pl.pallas_call(kernel, out_shape=pltpu.VMEM((1, SLAB, CROP), f32), in_spe...  41.5 us

profile of v2, /device:TPU:8, one launch (start us, length us, event | category | flops | bytes accessed | tf_op | source)
XLA Modules:
  0.0 42.2 jit_solution(18133985164387495627)
XLA Ops:
  0.0 41.5 %shard_map.64 = f32[1,64,1024]{2,1,0:T(8,128)S(1)} custom-call(s32[2,2]{1,0:T(2,128)} %centres.1, s32[16]{0:T(128)} %angle_index.1, s32[2,1,16]{2,1,0:T(1,128)} %offsets.1, bf16[2,128,2048]{2,1,0:T(8,128)(2,1)} %hologram.1, bf16[3584,256]{1,0:T(8,128)(2,1)} %constant.4.clone.x_hbm, bf16[256,1792]{1,0:T(8,128)(2,1)} %constant.5.clone.y_hbm), custom_call_target="tpu_custom_call" | custom-call | tf_op jit(solution)/shard_map/pallas_call | solution.py:402
  41.5 0.7 %copy.8 = f32[1,64,1024]{2,1,0:T(8,128)} copy(f32[1,64,1024]{2,1,0:T(8,128)S(1)} %shard_map.64) | data formatting | bytes 524288

commit v3 on v2

--- a/solution.py
+++ b/solution.py
@@ -82,18 +82,19 @@
     return lax.dot_general(a, b, (((1,), (1,)), ((), ())), preferred_element_type=f32)
 
 
-def kernel(centres, angle_index, offsets, hologram, x_hbm, y_hbm, out,
-           x_strip, y_strip, raw, q_tab, p_tab, odd, evens, even, send1, recv1, send2, recv2, rot, ryt, wave, back,
+def kernel(centres, angle_index, offsets, hologram_hbm, x_hbm, y_hbm, out,
+           hologram, x_strip, y_strip, raw, q_tab, p_tab, odd, evens, even, send1, recv1, send2, recv2, rot, ryt, wave, back,
            turn_tab, plane_tab, spread, own, send3, recv3, copy_sem, s1, r1, s2, r2, s3, r3):
     row = lax.axis_index("row")
     group = lax.axis_index("angle")
 
+    barrier = pltpu.get_barrier_semaphore()
+    h_copy = pltpu.make_async_copy(hologram_hbm, hologram, copy_sem.at[2])
     x_copy = pltpu.make_async_copy(x_hbm, x_strip, copy_sem.at[0])
     y_copy = pltpu.make_async_copy(y_hbm, y_strip, copy_sem.at[1])
+    h_copy.start()
     x_copy.start()
     y_copy.start()
-
-    barrier = pltpu.get_barrier_semaphore()
 
     def greet_row(i, carry):
         pl.semaphore_signal(barrier, inc=1, device_id={"row": lax.rem(row + i, ROWS)}, device_id_type=MESH)
@@ -143,17 +144,17 @@
                 im = z[2 * SLAB * h + SLAB:2 * SLAB * (h + 1), side * LANE:(side + 1) * LANE]
                 yield h, side, re * c - im * s, re * s + im * c
 
+    row_phases(0)
+    h_copy.wait()
     modulate(0, odd)
-    row_phases(0)
     x_copy.wait()
-    pl.semaphore_wait(barrier, ROWS + GROUPS - 2)
 
     def first_copy(to):
         return pltpu.make_async_remote_copy(
             src_ref=send1.at[to], dst_ref=recv1.at[row], send_sem=s1.at[0], recv_sem=r1.at[0],
             device_id={"row": to}, device_id_type=MESH)
 
-    def odd_rows(k, carry):
+    for k in range(2):
         pair = lax.rem(row // 4 + k, 2)
         for half in range(2):
             block = 2 * pair + half
@@ -162,6 +163,9 @@
                 send1[to, :, 0:LANE] = re.astype(bf16)
                 send1[to, :, LANE:WIDE] = im.astype(bf16)
 
+        if k == 0:
+            pl.semaphore_wait(barrier, ROWS + GROUPS - 2)
+
         def push(i, carry):
             to = SLABS * (i // 4) + 4 * pair + lax.rem(row + i, 4)
 
@@ -175,9 +179,6 @@
             return carry
 
         lax.fori_loop(0, 8, push, 0)
-        return carry
-
-    lax.fori_loop(0, 2, odd_rows, 0)
 
     def even_rows():
         modulate(1, evens)
@@ -402,9 +403,10 @@
     return pl.pallas_call(
         kernel,
         out_shape=pltpu.VMEM((1, SLAB, CROP), f32),
-        in_specs=[smem, smem, smem, vmem, anywhere, anywhere],
+        in_specs=[smem, smem, smem, anywhere, anywhere, anywhere],
         out_specs=vmem,
         scratch_shapes=[
+            pltpu.VMEM(hologram.shape, bf16),
             pltpu.VMEM(x_strip.shape, bf16),
             pltpu.VMEM(y_strip.shape, bf16),
             pltpu.VMEM((HELD, PIX // LANE, 2 * SLAB, LANE), f32),
@@ -427,7 +429,7 @@
             pltpu.VMEM((PLANES * HALF, TILE), f32),
             pltpu.VMEM((HALVES * TILES * GROUPS, HALF, TILE), bf16),
             pltpu.VMEM((HALVES * TILES * (GROUPS - 1), HALF, TILE), bf16),
-            pltpu.SemaphoreType.DMA((2,)),
+            pltpu.SemaphoreType.DMA((3,)),
             pltpu.SemaphoreType.DMA((1,)),
             pltpu.SemaphoreType.DMA((1,)),
             pltpu.SemaphoreType.DMA((HALVES,)),

time: 42.4 us -> 41 us (0.967)
  Pallas kernels: 41.5 us -> 40.1 us
    pallas_call x1, Pallas kernels: 41.5 us -> 40.1 us  [per_device(): pl.pallas_call(kernel, out_shape=pltpu.VMEM((1, SLAB, CROP), f32), in_spe...]
where the time goes in v3:
time: 41 us; the launch traced here: 40.8 us
  Pallas kernels  40.1 us (98%)
  local copies, waits for them, and re-layouts  0.71 us (2%)
    pallas_call x1, Pallas kernels, per_device(): pl.pallas_call(kernel, out_shape=pltpu.VMEM((1, SLAB, CROP), f32), in_spe...  40.1 us

profile of v3, /device:TPU:8, one launch (start us, length us, event | category | flops | bytes accessed | tf_op | source)
XLA Modules:
  0.0 40.8 jit_solution(6701349394195920573)
XLA Ops:
  0.0 40.1 %shard_map.64 = f32[1,64,1024]{2,1,0:T(8,128)S(1)} custom-call(s32[2,2]{1,0:T(2,128)} %centres.1, s32[16]{0:T(128)} %angle_index.1, s32[2,1,16]{2,1,0:T(1,128)} %offsets.1, bf16[2,128,2048]{2,1,0:T(8,128)(2,1)} %hologram_hbm.1, bf16[3584,256]{1,0:T(8,128)(2,1)} %constant.4.clone.x_hbm, bf16[256,1792]{1,0:T(8,128)(2,1)} %constant.5.clone.y_hbm), custom_call_target="tpu_custom_call" | custom-call | tf_op jit(solution)/shard_map/pallas_call | solution.py:403
  40.1 0.7 %copy.8 = f32[1,64,1024]{2,1,0:T(8,128)} copy(f32[1,64,1024]{2,1,0:T(8,128)S(1)} %shard_map.64) | data formatting | bytes 524288

commit v4 on v3

--- a/solution.py
+++ b/solution.py
@@ -82,8 +82,8 @@
     return lax.dot_general(a, b, (((1,), (1,)), ((), ())), preferred_element_type=f32)
 
 
-def kernel(centres, angle_index, offsets, hologram_hbm, x_hbm, y_hbm, out,
-           hologram, x_strip, y_strip, raw, q_tab, p_tab, odd, evens, even, send1, recv1, send2, recv2, rot, ryt, wave, back,
+def kernel(centres_hbm, angle_hbm, offsets_hbm, hologram_hbm, x_hbm, y_hbm, out,
+           centres, angle_index, offsets, hologram, x_strip, y_strip, raw, q_tab, p_tab, odd, evens, even, send1, recv1, send2, recv2, rot, ryt, wave, back,
            turn_tab, plane_tab, spread, own, send3, recv3, copy_sem, s1, r1, s2, r2, s3, r3):
     row = lax.axis_index("row")
     group = lax.axis_index("angle")
@@ -92,9 +92,6 @@
     h_copy = pltpu.make_async_copy(hologram_hbm, hologram, copy_sem.at[2])
     x_copy = pltpu.make_async_copy(x_hbm, x_strip, copy_sem.at[0])
     y_copy = pltpu.make_async_copy(y_hbm, y_strip, copy_sem.at[1])
-    h_copy.start()
-    x_copy.start()
-    y_copy.start()
 
     def greet_row(i, carry):
         pl.semaphore_signal(barrier, inc=1, device_id={"row": lax.rem(row + i, ROWS)}, device_id_type=MESH)
@@ -104,8 +101,20 @@
         pl.semaphore_signal(barrier, inc=1, device_id={"angle": lax.rem(group + i, GROUPS)}, device_id_type=MESH)
         return carry
 
+    small = [
+        pltpu.make_async_copy(centres_hbm, centres, copy_sem.at[3]),
+        pltpu.make_async_copy(angle_hbm, angle_index, copy_sem.at[4]),
+        pltpu.make_async_copy(offsets_hbm, offsets, copy_sem.at[5]),
+    ]
+    for copy in small:
+        copy.start()
+    h_copy.start()
+    x_copy.start()
     lax.fori_loop(1, ROWS, greet_row, 0)
     lax.fori_loop(1, GROUPS, greet_group, 0)
+    y_copy.start()
+    for copy in small:
+        copy.wait()
 
     at_x = LANE * iota((PIX // LANE, LANE), 0) + iota((PIX // LANE, LANE), 1)
     for h in range(HELD):
@@ -146,39 +155,40 @@
 
     row_phases(0)
     h_copy.wait()
+    x_copy.wait()
     modulate(0, odd)
-    x_copy.wait()
-
-    def first_copy(to):
+
+    def first_copy(part, to):
         return pltpu.make_async_remote_copy(
-            src_ref=send1.at[to], dst_ref=recv1.at[row], send_sem=s1.at[0], recv_sem=r1.at[0],
+            src_ref=send1.at[part, to], dst_ref=recv1.at[part, row], send_sem=s1.at[part], recv_sem=r1.at[part],
             device_id={"row": to}, device_id_type=MESH)
 
-    for k in range(2):
-        pair = lax.rem(row // 4 + k, 2)
-        for half in range(2):
-            block = 2 * pair + half
-            for h, side, re, im in across(odd, block):
-                to = SLABS * h + 2 * block + side
-                send1[to, :, 0:LANE] = re.astype(bf16)
-                send1[to, :, LANE:WIDE] = im.astype(bf16)
-
-        if k == 0:
-            pl.semaphore_wait(barrier, ROWS + GROUPS - 2)
-
-        def push(i, carry):
-            to = SLABS * (i // 4) + 4 * pair + lax.rem(row + i, 4)
-
-            @pl.when(to != row)
-            def _():
-                first_copy(to).start()
-
-            @pl.when(to == row)
-            def _():
-                recv1[row] = send1[row]
-            return carry
-
-        lax.fori_loop(0, 8, push, 0)
+    def first_all(part):
+        return pltpu.make_async_remote_copy(
+            src_ref=send1.at[part, 0:ROWS - 1], dst_ref=recv1.at[part, 0:ROWS - 1], send_sem=s1.at[part],
+            recv_sem=r1.at[part], device_id={"row": row}, device_id_type=MESH)
+
+    for block in range(4):
+        for h, side, re, im in across(odd, block):
+            to = SLABS * h + 2 * block + side
+            send1[0, to] = re.astype(bf16)
+            send1[1, to] = im.astype(bf16)
+
+    pl.semaphore_wait(barrier, ROWS + GROUPS - 2)
+
+    def push_real(i, carry):
+        first_copy(0, lax.rem(row + i, ROWS)).start()
+        return carry
+
+    lax.fori_loop(1, ROWS, push_real, 0)
+
+    def push_imag(i, carry):
+        first_copy(1, lax.rem(row + i, ROWS)).start()
+        return carry
+
+    lax.fori_loop(1, ROWS, push_imag, 0)
+    for part in range(2):
+        recv1[part, row] = send1[part, row]
 
     def even_rows():
         modulate(1, evens)
@@ -234,34 +244,38 @@
     table(lambda j: j * f32(1.0 / CROP), wave, 0)
 
     y_copy.wait()
-    pltpu.make_async_remote_copy(
-        src_ref=send1.at[0:ROWS - 1], dst_ref=recv1.at[0:ROWS - 1], send_sem=s1.at[0], recv_sem=r1.at[0],
-        device_id={"row": row}, device_id_type=MESH).wait_recv()
-
-    def second_copy(half, to):
+
+    def second_copy(half, part, to):
         return pltpu.make_async_remote_copy(
-            src_ref=send2.at[half, to], dst_ref=recv2.at[half, row], send_sem=s2.at[half], recv_sem=r2.at[half],
-            device_id={"row": to}, device_id_type=MESH)
-
-    def second_all(half):
+            src_ref=send2.at[half, part, to], dst_ref=recv2.at[half, part, row], send_sem=s2.at[half, part],
+            recv_sem=r2.at[half, part], device_id={"row": to}, device_id_type=MESH)
+
+    def second_all(half, part):
         return pltpu.make_async_remote_copy(
-            src_ref=send2.at[half, 0:ROWS - 1], dst_ref=recv2.at[half, 0:ROWS - 1], send_sem=s2.at[half],
-            recv_sem=r2.at[half], device_id={"row": row}, device_id_type=MESH)
-
-    gathered = recv1[...].reshape(CROP, WIDE)
-    for half in range(HALVES):
+            src_ref=send2.at[half, part, 0:ROWS - 1], dst_ref=recv2.at[half, part, 0:ROWS - 1],
+            send_sem=s2.at[half, part], recv_sem=r2.at[half, part], device_id={"row": row}, device_id_type=MESH)
+
+    def down(half, part):
+        gathered = recv1[part].reshape(CROP, LANE)
         for block in range(4):
             first = 3 * WIDE - WIDE * block
             z = dot(y_strip[half * 4 * HALF:(half + 1) * 4 * HALF, first:first + CROP], gathered).astype(bf16)
-            for part in range(4):
-                send2[half, 4 * block + part] = z[HALF * part:HALF * (part + 1), :]
+            for slab in range(4):
+                send2[half, part, 4 * block + slab] = z[HALF * slab:HALF * (slab + 1), :]
 
         def push(i, carry):
-            second_copy(half, lax.rem(row + i, ROWS)).start()
+            second_copy(half, part, lax.rem(row + i, ROWS)).start()
             return carry
 
         lax.fori_loop(1, ROWS, push, 0)
-        recv2[half, row] = send2[half, row]
+        recv2[half, part, row] = send2[half, part, row]
+
+    first_all(0).wait_recv()
+    down(0, 0)
+    first_all(1).wait_recv()
+    down(0, 1)
+    down(1, 0)
+    down(1, 1)
 
     back_table(0)
     back_table(1)
@@ -297,8 +311,8 @@
             c = rot[0, rows, lanes]
             s = rot[1, rows, lanes]
             for h in range(HELD):
-                re = even[2 * h, rows, lanes] + recv2[half, SLABS * h + slab, :, 0:LANE].astype(f32)
-                im = even[2 * h + 1, rows, lanes] + recv2[half, SLABS * h + slab, :, LANE:WIDE].astype(f32)
+                re = even[2 * h, rows, lanes] + recv2[half, 0, SLABS * h + slab].astype(f32)
+                im = even[2 * h + 1, rows, lanes] + recv2[half, 1, SLABS * h + slab].astype(f32)
                 field_re = re * c - im * s
                 field_im = re * s + im * c
                 energy = field_re * field_re + field_im * field_im + 1.0
@@ -367,7 +381,8 @@
             out[0, half * HALF:(half + 1) * HALF, lanes] = own[pl.ds(pl.multiple_of(HALF * group, HALF), HALF), :]
 
     for half in range(HALVES):
-        second_all(half).wait_recv()
+        second_all(half, 0).wait_recv()
+        second_all(half, 1).wait_recv()
         rytov(half)
         filtered(half)
         planes(half)
@@ -384,12 +399,10 @@
             total = total + recv3[first + j].astype(f32)
         out[0, rows, lanes] = total
 
-    first_all = pltpu.make_async_remote_copy(
-        src_ref=send1.at[0:ROWS - 1], dst_ref=recv1.at[0:ROWS - 1], send_sem=s1.at[0], recv_sem=r1.at[0],
-        device_id={"row": row}, device_id_type=MESH)
-    first_all.wait_send()
-    for half in range(HALVES):
-        second_all(half).wait_send()
+    for part in range(2):
+        first_all(part).wait_send()
+        for half in range(HALVES):
+            second_all(half, part).wait_send()
     count = HALVES * TILES * (GROUPS - 1)
     pltpu.make_async_remote_copy(
         src_ref=send3.at[0:count], dst_ref=recv3.at[0:count], send_sem=s3.at[0], recv_sem=r3.at[0],
@@ -397,15 +410,17 @@
 
 
 def per_device(x_strip, y_strip, hologram, centres, offsets, angle_index):
-    smem = pl.BlockSpec(memory_space=pltpu.SMEM)
     vmem = pl.BlockSpec(memory_space=pltpu.VMEM)
     anywhere = pl.BlockSpec(memory_space=pl.ANY)
     return pl.pallas_call(
         kernel,
         out_shape=pltpu.VMEM((1, SLAB, CROP), f32),
-        in_specs=[smem, smem, smem, anywhere, anywhere, anywhere],
+        in_specs=[anywhere] * 6,
         out_specs=vmem,
         scratch_shapes=[
+            pltpu.SMEM(centres.shape, jnp.int32),
+            pltpu.SMEM(angle_index.shape, jnp.int32),
+            pltpu.SMEM(offsets.shape, jnp.int32),
             pltpu.VMEM(hologram.shape, bf16),
             pltpu.VMEM(x_strip.shape, bf16),
             pltpu.VMEM(y_strip.shape, bf16),
@@ -415,10 +430,10 @@
             pltpu.VMEM((2 * HELD * SLAB, PIX), bf16),
             pltpu.VMEM((2 * HELD * SLAB, PIX), bf16),
             pltpu.VMEM((2 * HELD, SLAB, CROP), f32),
-            pltpu.VMEM((ROWS, SLAB, WIDE), bf16),
-            pltpu.VMEM((ROWS, SLAB, WIDE), bf16),
-            pltpu.VMEM((HALVES, ROWS, HALF, WIDE), bf16),
-            pltpu.VMEM((HALVES, ROWS, HALF, WIDE), bf16),
+            pltpu.VMEM((2, ROWS, SLAB, LANE), bf16),
+            pltpu.VMEM((2, ROWS, SLAB, LANE), bf16),
+            pltpu.VMEM((HALVES, 2, ROWS, HALF, LANE), bf16),
+            pltpu.VMEM((HALVES, 2, ROWS, HALF, LANE), bf16),
             pltpu.VMEM((2, SLAB, CROP), f32),
             pltpu.VMEM((HALVES, 2 * HELD * HALF, CROP), bf16),
             pltpu.VMEM((CROP, 2 * CROP), bf16),
@@ -429,11 +444,11 @@
             pltpu.VMEM((PLANES * HALF, TILE), f32),
             pltpu.VMEM((HALVES * TILES * GROUPS, HALF, TILE), bf16),
             pltpu.VMEM((HALVES * TILES * (GROUPS - 1), HALF, TILE), bf16),
-            pltpu.SemaphoreType.DMA((3,)),
-            pltpu.SemaphoreType.DMA((1,)),
-            pltpu.SemaphoreType.DMA((1,)),
-            pltpu.SemaphoreType.DMA((HALVES,)),
-            pltpu.SemaphoreType.DMA((HALVES,)),
+            pltpu.SemaphoreType.DMA((6,)),
+            pltpu.SemaphoreType.DMA((2,)),
+            pltpu.SemaphoreType.DMA((2,)),
+            pltpu.SemaphoreType.DMA((HALVES, 2)),
+            pltpu.SemaphoreType.DMA((HALVES, 2)),
             pltpu.SemaphoreType.DMA((1,)),
             pltpu.SemaphoreType.DMA((HALVES * TILES,)),
         ],

time: 41 us -> 40.1 us (0.978)
  Pallas kernels: 40.1 us -> 39.2 us
    pallas_call x1, Pallas kernels: 40.1 us -> 39.2 us  [per_device(): pl.pallas_call(kernel, out_shape=pltpu.VMEM((1, SLAB, CROP), f32), in_spe...]
where the time goes in v4:
time: 40.1 us; the launch traced here: 39.9 us
  Pallas kernels  39.2 us (98%)
  local copies, waits for them, and re-layouts  0.71 us (2%)
    pallas_call x1, Pallas kernels, per_device(): pl.pallas_call(kernel, out_shape=pltpu.VMEM((1, SLAB, CROP), f32), in_spe...  39.2 us

profile of v4, /device:TPU:8, one launch (start us, length us, event | category | flops | bytes accessed | tf_op | source)
XLA Modules:
  0.0 39.9 jit_solution(4546139225025265495)
XLA Ops:
  0.0 39.2 %shard_map.64 = f32[1,64,1024]{2,1,0:T(8,128)S(1)} custom-call(s32[2,2]{1,0:T(2,128)} %centres_hbm.1, s32[16]{0:T(128)} %angle_hbm.1, s32[2,1,16]{2,1,0:T(1,128)} %offsets_hbm.1, bf16[2,128,2048]{2,1,0:T(8,128)(2,1)} %hologram_hbm.1, bf16[3584,256]{1,0:T(8,128)(2,1)} %constant.4.clone.x_hbm, bf16[256,1792]{1,0:T(8,128)(2,1)} %constant.5.clone.y_hbm), custom_call_target="tpu_custom_call" | custom-call | tf_op jit(solution)/shard_map/pallas_call | solution.py:415
  39.2 0.7 %copy.8 = f32[1,64,1024]{2,1,0:T(8,128)} copy(f32[1,64,1024]{2,1,0:T(8,128)S(1)} %shard_map.64) | data formatting | bytes 524288

commit v5 on v4

--- a/solution.py
+++ b/solution.py
@@ -243,43 +243,6 @@
 
     table(lambda j: j * f32(1.0 / CROP), wave, 0)
 
-    y_copy.wait()
-
-    def second_copy(half, part, to):
-        return pltpu.make_async_remote_copy(
-            src_ref=send2.at[half, part, to], dst_ref=recv2.at[half, part, row], send_sem=s2.at[half, part],
-            recv_sem=r2.at[half, part], device_id={"row": to}, device_id_type=MESH)
-
-    def second_all(half, part):
-        return pltpu.make_async_remote_copy(
-            src_ref=send2.at[half, part, 0:ROWS - 1], dst_ref=recv2.at[half, part, 0:ROWS - 1],
-            send_sem=s2.at[half, part], recv_sem=r2.at[half, part], device_id={"row": row}, device_id_type=MESH)
-
-    def down(half, part):
-        gathered = recv1[part].reshape(CROP, LANE)
-        for block in range(4):
-            first = 3 * WIDE - WIDE * block
-            z = dot(y_strip[half * 4 * HALF:(half + 1) * 4 * HALF, first:first + CROP], gathered).astype(bf16)
-            for slab in range(4):
-                send2[half, part, 4 * block + slab] = z[HALF * slab:HALF * (slab + 1), :]
-
-        def push(i, carry):
-            second_copy(half, part, lax.rem(row + i, ROWS)).start()
-            return carry
-
-        lax.fori_loop(1, ROWS, push, 0)
-        recv2[half, part, row] = send2[half, part, row]
-
-    first_all(0).wait_recv()
-    down(0, 0)
-    first_all(1).wait_recv()
-    down(0, 1)
-    down(1, 0)
-    down(1, 1)
-
-    back_table(0)
-    back_table(1)
-
     spatial = (LANE * iota((SLABS, LANE), 0) + iota((SLABS, LANE), 1) - CROP // 2).astype(f32) * f32(1.0 / CROP)
     ramp = jnp.abs(spatial) * f32(2.0 / math.sqrt(CROP * HOLOS) / math.sqrt(CROP))
     for h in range(HELD):
@@ -300,6 +263,48 @@
         return carry
 
     lax.fori_loop(0, SLABS, rotations, 0)
+
+    y_copy.wait()
+
+    def second_copy(half, part, to):
+        return pltpu.make_async_remote_copy(
+            src_ref=send2.at[half, part, to], dst_ref=recv2.at[half, part, row], send_sem=s2.at[half, part],
+            recv_sem=r2.at[half, part], device_id={"row": to}, device_id_type=MESH)
+
+    def second_all(half, part):
+        return pltpu.make_async_remote_copy(
+            src_ref=send2.at[half, part, 0:ROWS - 1], dst_ref=recv2.at[half, part, 0:ROWS - 1],
+            send_sem=s2.at[half, part], recv_sem=r2.at[half, part], device_id={"row": row}, device_id_type=MESH)
+
+    def down(half, part):
+        gathered = recv1[part].reshape(CROP, LANE)
+        for block in range(4):
+            first = 3 * WIDE - WIDE * block
+            z = dot(y_strip[half * 4 * HALF:(half + 1) * 4 * HALF, first:first + CROP], gathered).astype(bf16)
+            for slab in range(4):
+                send2[half, part, 4 * block + slab] = z[HALF * slab:HALF * (slab + 1), :]
+
+        recv2[half, part, row] = send2[half, part, row]
+
+    def push_second(half, part):
+        def push(i, carry):
+            second_copy(half, part, lax.rem(row + i, ROWS)).start()
+            return carry
+
+        lax.fori_loop(1, ROWS, push, 0)
+
+    back_table(0)
+    first_all(0).wait_recv()
+    down(0, 0)
+    push_second(0, 0)
+    down(1, 0)
+    first_all(1).wait_recv()
+    down(0, 1)
+    push_second(0, 1)
+    push_second(1, 0)
+    down(1, 1)
+    push_second(1, 1)
+    back_table(1)
 
     left_half = iota((HALF, LANE), 1) < BLOCK
 
@@ -324,7 +329,7 @@
                 ryt[half, at + HALF:at + 2 * HALF, lanes] = turned.astype(bf16)
             return carry
 
-        lax.fori_loop(0, SLABS, slab_of, 0)
+        lax.fori_loop(0, SLABS, slab_of, 0, unroll=4)
 
     def filtered(half):
         for k in range(CROP // WIDE):

time: 40.1 us -> 39.8 us (level)
  no operation moved by 1% of the time
where the time goes in v5:
time: 39.8 us; the launch traced here: 39.7 us
  Pallas kernels  39 us (98%)
  local copies, waits for them, and re-layouts  0.71 us (2%)
    pallas_call x1, Pallas kernels, per_device(): pl.pallas_call(kernel, out_shape=pltpu.VMEM((1, SLAB, CROP), f32), in_spe...  39 us

profile of v5, /device:TPU:8, one launch (start us, length us, event | category | flops | bytes accessed | tf_op | source)
XLA Modules:
  0.0 39.7 jit_solution(9873068236033286373)
XLA Ops:
  0.0 39.0 %shard_map.64 = f32[1,64,1024]{2,1,0:T(8,128)S(1)} custom-call(s32[2,2]{1,0:T(2,128)} %centres_hbm.1, s32[16]{0:T(128)} %angle_hbm.1, s32[2,1,16]{2,1,0:T(1,128)} %offsets_hbm.1, bf16[2,128,2048]{2,1,0:T(8,128)(2,1)} %hologram_hbm.1, bf16[3584,256]{1,0:T(8,128)(2,1)} %constant.4.clone.x_hbm, bf16[256,1792]{1,0:T(8,128)(2,1)} %constant.5.clone.y_hbm), custom_call_target="tpu_custom_call" | custom-call | tf_op jit(solution)/shard_map/pallas_call | solution.py:420
  39.0 0.7 %copy.8 = f32[1,64,1024]{2,1,0:T(8,128)} copy(f32[1,64,1024]{2,1,0:T(8,128)S(1)} %shard_map.64) | data formatting | bytes 524288

commit v6 on v5

--- a/solution.py
+++ b/solution.py
@@ -106,12 +106,12 @@
         pltpu.make_async_copy(angle_hbm, angle_index, copy_sem.at[4]),
         pltpu.make_async_copy(offsets_hbm, offsets, copy_sem.at[5]),
     ]
+    h_copy.start()
+    lax.fori_loop(1, ROWS, greet_row, 0, unroll=True)
+    lax.fori_loop(1, GROUPS, greet_group, 0, unroll=True)
     for copy in small:
         copy.start()
-    h_copy.start()
     x_copy.start()
-    lax.fori_loop(1, ROWS, greet_row, 0)
-    lax.fori_loop(1, GROUPS, greet_group, 0)
     y_copy.start()
     for copy in small:
         copy.wait()

time: 39.8 us -> 39.9 us (level)
  no operation moved by 1% of the time
where the time goes in v6:
time: 39.9 us; the launch traced here: 39.7 us
  Pallas kernels  39 us (98%)
  local copies, waits for them, and re-layouts  0.71 us (2%)
    pallas_call x1, Pallas kernels, per_device(): pl.pallas_call(kernel, out_shape=pltpu.VMEM((1, SLAB, CROP), f32), in_spe...  39 us

profile of v6, /device:TPU:8, one launch (start us, length us, event | category | flops | bytes accessed | tf_op | source)
XLA Modules:
  0.0 39.7 jit_solution(14220987195897701029)
XLA Ops:
  0.0 39.0 %shard_map.64 = f32[1,64,1024]{2,1,0:T(8,128)S(1)} custom-call(s32[2,2]{1,0:T(2,128)} %centres_hbm.1, s32[16]{0:T(128)} %angle_hbm.1, s32[2,1,16]{2,1,0:T(1,128)} %offsets_hbm.1, bf16[2,128,2048]{2,1,0:T(8,128)(2,1)} %hologram_hbm.1, bf16[3584,256]{1,0:T(8,128)(2,1)} %constant.4.clone.x_hbm, bf16[256,1792]{1,0:T(8,128)(2,1)} %constant.5.clone.y_hbm), custom_call_target="tpu_custom_call" | custom-call | tf_op jit(solution)/shard_map/pallas_call | solution.py:420
  39.0 0.7 %copy.8 = f32[1,64,1024]{2,1,0:T(8,128)} copy(f32[1,64,1024]{2,1,0:T(8,128)S(1)} %shard_map.64) | data formatting | bytes 524288
